TPU v7x, 128 devices: a whole 4x4x4 slice. The times are simulated.
128 devices in a mesh: row: 8 (over y, core), col: 16 (over z, x).
Axes of the slice: x: 4, y: 4, z: 4, core: 2. Of those that a mesh axis runs over, the one named last changes fastest.
Arguments:
- factor: float32 [256, 1536, 1536], P(('row', 'col'))
- coupling: bfloat16 [256, 1536, 512], P(('row', 'col')), may hold values from -0.15625 to 0.15625
- boundary: float32 [256, 512, 512], P(('row', 'col'))
- loads: float32 [32, 16384], P(None, ('row', 'col')), may hold values from -6 to 6
- block_ids: int32 [256, 16], P(('row', 'col')), may hold values from 0 to 511, as said below
- live_counts: int32 [256], P(('row', 'col')), may hold values from 8 to 16
Outputs:
- response: float32 [32, 16384], P(None, ('row', 'col'))
Inputs may be any that keep to these rules, and one draw needn't show every extreme that they name: `block_ids`: district d lies on device d // 2 (rows then columns of the mesh); its slot s names a block owned by the device in the same mesh row and in mesh column s % 16, where device p owns blocks p * 4 to p * 4 + 3.
All inputs are finite; a program needn't handle non-finite values.
Results may differ from a plain program's by a relative error of at most 0.0003.
Values sent between devices are 32-bit elements; how exact they have to be, the bound alone decides.
No kernel may reach another device: no remote copies, remote signals or barrier semaphores. Data moves between devices by JAX's collectives and lax.ppermute only.
A program may use at most 128 MiB of HBM per device.

v0:
```python
import jax
import jax.numpy as jnp
from jax import lax
from jax.sharding import PartitionSpec as P

BS = 32


def district_image(factor, coupling, boundary, picked, live_count):
    solved = jax.scipy.linalg.solve_triangular(factor, coupling.astype(jnp.float32), lower=True)
    schur_block = boundary - lax.dot_general(
        solved,
        solved,
        (((0,), (0,)), ((), ())),
        precision=lax.Precision.HIGHEST,
        preferred_element_type=jnp.float32,
    )
    weights = (jnp.arange(picked.shape[1]) < live_count).astype(jnp.float32)
    masked = (picked * weights[None, :, None]).reshape(picked.shape[0], -1)
    image = lax.dot_general(
        masked,
        schur_block,
        (((1,), (1,)), ((), ())),
        precision=lax.Precision.HIGHEST,
        preferred_element_type=jnp.float32,
    )
    return image.reshape(picked.shape) * weights[None, :, None]


def body(factor, coupling, boundary, loads, block_ids, live_counts):
    cases = loads.shape[0]
    gathered = lax.all_gather(loads, "col", axis=1, tiled=True)
    offset = lax.axis_index("row") * (gathered.shape[1] // BS)
    load_table = gathered.reshape(cases, -1, BS)
    images = []
    for district in range(factor.shape[0]):
        picked = jnp.take(load_table, block_ids[district] - offset, axis=1)
        images.append(
            district_image(
                factor[district],
                coupling[district],
                boundary[district],
                picked,
                live_counts[district],
            )
        )
    images = jnp.concatenate(images, axis=1)
    flat_ids = block_ids.reshape(-1)
    block_total = load_table.shape[1]
    onehot = ((flat_ids - offset)[:, None] == jnp.arange(block_total)[None, :]).astype(jnp.float32)
    dense_term = jnp.einsum("rsb,sj->rjb", images, onehot, precision=lax.Precision.HIGHEST).reshape(
        cases, -1
    )
    return lax.psum_scatter(dense_term, "col", scatter_dimension=1, tiled=True)


def solution(mesh):
    placed = (
        P(("row", "col"), None, None),
        P(("row", "col"), None, None),
        P(("row", "col"), None, None),
        P(None, ("row", "col")),
        P(("row", "col"), None),
        P(("row", "col")),
    )
    return jax.shard_map(
        body, mesh=mesh, in_specs=placed, out_specs=P(None, ("row", "col")), check_vma=False
    )
```

profile of v0, /device:TPU:0, one launch (start us, length us, event | category | flops | bytes accessed | tf_op | source)
XLA Modules:
  0.0 552.0 jit_solution(11103956469716437403)
XLA Ops:
  8.0 14.9 %bitcast_select_fusion.1 = (f32[1536,1536]{1,0:T(8,128)}, f32[1536,1536]{1,0:T(8,128)}) fusion(f32[2,1536,1536]{2,1,0:T(8,128)} %param.10), kind=kLoop, calls=%fused_computation.7 | loop fusion | flops 7077888 | bytes 37748736 | tf_op jit(solution)/shard_map/jit(_solve_triangular)/triangular_solve | solution.py:10
  23.9 40.8 %while.4 = (s32[]{:T(128)}, f32[1536,1536]{1,0:T(8,128)}, s32[12,2]{0,1:T(2,128)S(1)}, f32[12,128,128]{2,1,0:T(8,128)}, s32[]{:T(128)}) while((s32[]{:T(128)}, f32[1536,1536]{1,0:T(8,128)}, s32[12,2]{0,1:T(2,128)S(1)}, f32[12,128,128]{2,1,0:T(8,128)}, s32[]{:T(128)}) %tuple.167), condition=%wide.while_cond, body=%wide.while_body.sunk | while | flops 2 | bytes 132705 | solution.py:10
  64.7 119.5 %custom-call.4 = f32[12,128,128]{1,2,0:T(8,128)} custom-call(f32[12,128,128]{2,1,0:T(8,128)} %get-tuple-element.21), custom_call_target="InvertDiagBlocksLowerTriangular" | custom-call | tf_op jit(solution)/shard_map/jit(_solve_triangular)/triangular_solve | solution.py:10
  208.9 3.1 convolution_subtract_fusion.22
  212.4 3.6 convolution_subtract_fusion.8
  216.0 25.4 %all_gather.3 = f32[32,2048]{1,0:T(8,128)S(1)} all-gather(f32[32,128]{1,0:T(8,128)S(1)} %copy-done.7), channel_id=1, replica_groups=mesh['row'=8,'col'=16] {'col'}, dimensions={1}, use_global_device_ids=true | all-gather | bytes 278528 | tf_op jit(solution)/shard_map/all_gather | solution.py:32
  258.2 6.4 %convolution_subtract_fusion.1 = f32[512,512]{1,0:T(8,128)S(1)} fusion(f32[1536,512]{1,0:T(8,128)S(1)} %convolution_dynamic-update-slice_fusion.1, f32[2,512,512]{2,1,0:T(8,128)} %param.12), kind=kOutput, calls=%fused_computation.12 | convolution fusion | flops 4832100352 | bytes 8388608 | tf_op jit(solution)/shard_map/dot_general | solution.py:11
  271.0 42.2 %while.5 = (s32[]{:T(128)}, f32[1536,1536]{1,0:T(8,128)}, s32[12,2]{0,1:T(2,128)S(1)}, f32[12,128,128]{2,1,0:T(8,128)}, s32[]{:T(128)}) while((s32[]{:T(128)}, f32[1536,1536]{1,0:T(8,128)}, s32[12,2]{0,1:T(2,128)S(1)}, f32[12,128,128]{2,1,0:T(8,128)}, s32[]{:T(128)}) %tuple.172), condition=%wide.while_cond.clone, body=%wide.while_body.clone.sunk | while | flops 2 | bytes 132705 | solution.py:10
  271.6 2.9 bitcast_dynamic-update-slice_fusion.5
  275.1 2.9 bitcast_dynamic-update-slice_fusion.5
  278.7 2.9 bitcast_dynamic-update-slice_fusion.5
  282.2 2.9 bitcast_dynamic-update-slice_fusion.5
  285.7 2.9 bitcast_dynamic-update-slice_fusion.5
  289.2 2.9 bitcast_dynamic-update-slice_fusion.5
  292.7 2.9 bitcast_dynamic-update-slice_fusion.5
  296.3 2.9 bitcast_dynamic-update-slice_fusion.5
  299.8 2.9 bitcast_dynamic-update-slice_fusion.5
  303.3 2.9 bitcast_dynamic-update-slice_fusion.5
  306.8 2.9 bitcast_dynamic-update-slice_fusion.5
  313.2 119.5 %custom-call.5 = f32[12,128,128]{1,2,0:T(8,128)} custom-call(f32[12,128,128]{2,1,0:T(8,128)} %get-tuple-element.22), custom_call_target="InvertDiagBlocksLowerTriangular" | custom-call | tf_op jit(solution)/shard_map/jit(_solve_triangular)/triangular_solve | solution.py:10
  455.6 2.9 convolution_subtract_fusion.20
  459.0 3.1 convolution_subtract_fusion.2
  462.5 5.4 convolution_subtract_fusion
  473.3 71.6 %reduce-scatter.2.cloned.1.call-done = f32[32,128]{1,0:T(8,128)} async-done(((f32[32,2048]{1,0:T(8,128)}), f32[32,128]{1,0:T(8,128)}) %reduce-scatter.2.cloned.1.call-update) | async-done | bytes 16400 | tf_op jit(solution)/shard_map/reduce_scatter | solution.py:54
  (157 shorter events, 130.5 us)
Async XLA Ops:
  6.5 538.4 %reduce-scatter.2.cloned.1.call-start = ((), (), s32[]{:S(2)}) async-start(), calls=%async_computation.1 | async-start | bytes 278528 | tf_op jit(solution)/shard_map/reduce_scatter | solution.py:54
  8.0 176.2 %copy-start.1 = (bf16[2,1536,512]{2,1,0:T(8,128)(2,1)S(1)}, bf16[2,1536,512]{2,1,0:T(8,128)(2,1)}, u32[]{:S(2)}) copy-start(bf16[2,1536,512]{2,1,0:T(8,128)(2,1)} %param.11) | copy-start | bytes 9437188
  184.2 2.6 copy-start.5
  212.0 4.1 copy-start.7
  242.7 8.5 %copy-start.8 = (s32[2]{0:T(128)S(1)}, s32[2]{0:T(128)}, u32[]{:S(2)}) copy-start(s32[2]{0:T(128)} %param.15) | copy-start | bytes 28
  264.6 168.1 %copy-start = (f32[1536,512]{1,0:T(8,128)S(1)}, f32[1536,512]{1,0:T(8,128)}, u32[]{:S(2)}) copy-start(f32[1536,512]{1,0:T(8,128)} %get-tuple-element.50) | copy-start | bytes 9437188
  432.7 2.7 copy-start.6
  458.5 4.0 copy-start.4
  462.5 5.4 copy-start.2
  467.9 3.2 copy-start.3
Sparse Core Ops, SparseCore 0:
  473.5 71.3 reduce-scatter.1
where the time goes:
time: 557 us; the launch traced here: 552 us
  other arithmetic  264 us (47%)
  local copies, waits for them, and re-layouts  100 us (18%)
  matrix products  77.2 us (14%)
  waiting for transfers between devices  71.6 us (13%)
  blocking collectives  25.4 us (5%)
  between operations  14.2 us (3%)
    another operation x4, other arithmetic, district_image(): jax.scipy.linalg.solve_triangular(factor, coupling.astype(jnp.float32), l...  254 us
    another operation x75, local copies, waits for them, and re-layouts, district_image(): jax.scipy.linalg.solve_triangular(factor, coupling.astype(jnp.float32), l...  84.9 us
    reduce_scatter x1, waiting for transfers between devices, body(): return lax.psum_scatter(dense_term, 'col', scatter_dimension=1, tiled=True)  71.6 us
    another operation x46, matrix products, district_image(): jax.scipy.linalg.solve_triangular(factor, coupling.astype(jnp.float32), l...  60 us
    all_gather x1, blocking collectives, body(): gathered = lax.all_gather(loads, 'col', axis=1, tiled=True)  25.4 us
    dot_general x2, matrix products, district_image(): lax.dot_general(solved, solved, (((0,), (0,)), ((), ())), precision=lax.P...  11.8 us
  transfers between devices with their start and end apart: 1, of which 1 were waited for; matrix products, arithmetic and copies ran while one was open for 0% of the time, Pallas kernels for 0%

commit v1 on v0

v1 whole, which is shorter than its diff:
```python
import jax
import jax.numpy as jnp
from jax import lax
from jax.experimental import pallas as pl
from jax.experimental.pallas import tpu as pltpu
from jax.sharding import PartitionSpec as P

BS = 32
TILE = 256
HALF = TILE // 2
BASE = 32
LANES = 128
BF = jnp.bfloat16
F32 = jnp.float32


def split(a):
    high = a.astype(BF)
    return high, (a - high.astype(F32)).astype(BF)


def dot(a, b):
    return jnp.dot(a, b, preferred_element_type=F32)


def dot_t(a, b):
    return lax.dot_general(a, b, (((1,), (1,)), ((), ())), preferred_element_type=F32)


def dot3(a, b):
    both = dot(jnp.concatenate([a[0], a[1]], axis=1), jnp.concatenate([b[0], b[0]], axis=0))
    return both + dot(a[0], b[1])


def base_inverse(tile):
    lane = lax.broadcasted_iota(jnp.int32, (BASE, LANES), 1)
    row = lax.broadcasted_iota(jnp.int32, (BASE, LANES), 0)
    group, column = lane // BASE, lane % BASE
    packed = tile[:BASE]
    for b in range(1, LANES // BASE):
        packed = jnp.where(group == b, tile[b * BASE : (b + 1) * BASE], packed)
    diagonal = jnp.sum(jnp.where(row == column, packed, 0.0), axis=0, keepdims=True)
    recip = 1.0 / diagonal
    unit = jnp.where(row > column, packed * recip, 0.0)
    acc = jnp.where(row == column, 1.0, 0.0).astype(F32)
    parts = [acc[8 * g : 8 * g + 8] for g in range(BASE // 8)]
    for j in range(BASE - 1):
        pivot = parts[j // 8][j % 8 : j % 8 + 1]
        for g in range((j + 1) // 8, BASE // 8):
            index = group[:8] * BASE + j
            factor = jnp.take_along_axis(unit[8 * g : 8 * g + 8], index, axis=1)
            parts[g] = parts[g] - factor * pivot
    rows_scale = jnp.take_along_axis(
        jnp.broadcast_to(recip, (BASE, LANES)), group * BASE + row, axis=1
    )
    inverse = jnp.concatenate(parts, axis=0) * rows_scale
    return jnp.concatenate(
        [jnp.where(group == b, inverse, 0.0) for b in range(LANES // BASE)], axis=0
    )


def prepare_kernel(factor_ref, high_ref, low_ref, ihigh_ref, ilow_ref, held, inv, sem):
    districts, size, _ = factor_ref.shape
    steps = size // TILE
    diag, panels = {}, {}
    for d in range(districts):
        for k in range(steps):
            at = (d, pl.ds(k * TILE, TILE), pl.ds(k * TILE, TILE))
            diag[d, k] = pltpu.make_async_copy(factor_ref.at[at], held.at[at], sem.at[0, d, k])
            diag[d, k].start()
    for d in range(districts):
        for k in range(1, steps):
            at = (d, pl.ds(k * TILE, TILE), pl.ds(0, k * TILE))
            panels[d, k] = pltpu.make_async_copy(factor_ref.at[at], held.at[at], sem.at[1, d, k])
            panels[d, k].start()

    row = lax.broadcasted_iota(jnp.int32, (LANES, LANES), 0)
    col = lax.broadcasted_iota(jnp.int32, (LANES, LANES), 1)
    tiles = [(d, k, t) for d in range(districts) for k in range(steps) for t in range(2)]

    def tile_at(d, k, t, u):
        return held[d, pl.ds(k * TILE + t * HALF, HALF), pl.ds(k * TILE + u * HALF, HALF)]

    for d, k, t in tiles:
        if t == 0:
            diag[d, k].wait()
        inv[2 * (d * steps + k) + t] = base_inverse(tile_at(d, k, t, t))
    width = BASE
    while width < HALF:
        mask = (
            (row // (2 * width) == col // (2 * width))
            & (row % (2 * width) >= width)
            & (col % (2 * width) < width)
        )
        for d, k, t in tiles:
            at = 2 * (d * steps + k) + t
            x = inv[at]
            pair = split(x)
            off = split(jnp.where(mask, tile_at(d, k, t, t), 0.0))
            inv[at] = x - dot3(pair, split(dot3(off, pair)))
        width *= 2
    for d in range(districts):
        for k in range(steps):
            at = d * steps + k
            top, bottom = split(inv[2 * at]), split(inv[2 * at + 1])
            off = split(tile_at(d, k, 1, 0))
            left = split(-dot3(bottom, split(dot3(off, top))))
            zero = jnp.zeros((HALF, HALF), BF)
            for ref, i in ((ihigh_ref, 0), (ilow_ref, 1)):
                ref[at, :HALF, :HALF] = top[i]
                ref[at, :HALF, HALF:] = zero
                ref[at, HALF:, :HALF] = left[i]
                ref[at, HALF:, HALF:] = bottom[i]
    for d in range(districts):
        for k in range(1, steps):
            panels[d, k].wait()
            cols = k * TILE

            @pl.loop(0, TILE // 32)
            def _(i):
                at = (d, pl.ds(pl.multiple_of(k * TILE + i * 32, 32), 32), slice(0, cols))
                high, low = split(held[at])
                high_ref[at] = high
                low_ref[at] = low


def prepare(factor):
    districts, size, _ = factor.shape
    steps = size // TILE
    halves = jax.ShapeDtypeStruct((districts, size, size), BF)
    blocks = jax.ShapeDtypeStruct((districts * steps, TILE, TILE), BF)
    whole = pl.BlockSpec(memory_space=pltpu.VMEM)
    return pl.pallas_call(
        prepare_kernel,
        out_shape=(halves, halves, blocks, blocks),
        in_specs=[pl.BlockSpec(memory_space=pl.ANY)],
        out_specs=(whole,) * 4,
        scratch_shapes=[
            pltpu.VMEM((districts, size, size), F32),
            pltpu.VMEM((districts * steps * 2, LANES, LANES), F32),
            pltpu.SemaphoreType.DMA((2, districts, steps)),
        ],
        compiler_params=pltpu.CompilerParams(vmem_limit_bytes=24 << 20),
        cost_estimate=pl.CostEstimate(
            flops=20 * 10**9, bytes_accessed=12 << 20, transcendentals=0
        ),
        name="prepare",
    )(factor)


def apply_kernel(
    ids_ref,
    live_ref,
    gathered_ref,
    coupling_ref,
    boundary_ref,
    high_ref,
    low_ref,
    ihigh_ref,
    ilow_ref,
    out_ref,
):
    slots, cases, _ = gathered_ref.shape
    districts, size, faces = coupling_ref.shape
    steps = size // TILE
    per = LANES // BS
    group = lax.broadcasted_iota(jnp.int32, (cases, LANES), 1) // BS

    def stack(a):
        return jnp.concatenate(split(a), axis=0)

    def fold(a):
        return a[:cases] + a[cases:]

    masked, total, rest = [], [], []
    for d in range(districts):
        columns = []
        for tile in range(slots // per):
            acc = jnp.zeros((cases, LANES), F32)
            for g in range(per):
                s = tile * per + g
                within = ids_ref[d, s] % per
                piece = pltpu.roll(gathered_ref[s], ((g + per - within) % per) * BS, 1)
                acc = jnp.where((group == g) & (s < live_ref[d]), piece, acc)
            columns.append(acc)
        x = stack(jnp.concatenate(columns, axis=1))
        masked.append(x)
        right = dot_t(x, coupling_ref[d])
        rest.append([fold(right[:, k * TILE : (k + 1) * TILE]) for k in range(steps)])
        high, low = split(boundary_ref[d])
        total.append(fold(dot_t(x, high) + dot_t(x, low)))
    forward = [[None] * steps for _ in range(districts)]
    for k in range(steps):
        for d in range(districts):
            r = stack(rest[d][k])
            at = d * steps + k
            u = fold(dot_t(r, ihigh_ref[at]) + dot_t(r, ilow_ref[at]))
            forward[d][k] = u
            pair = stack(u)
            for j in range(k + 1, steps):
                block = (d, slice(j * TILE, (j + 1) * TILE), slice(k * TILE, (k + 1) * TILE))
                step = dot_t(pair, high_ref[block]) + dot_t(pair, low_ref[block])
                rest[d][j] = rest[d][j] - fold(step)
    for k in reversed(range(steps)):
        for d in range(districts):
            r = stack(forward[d][k])
            at = d * steps + k
            v = fold(dot(r, ihigh_ref[at]) + dot(r, ilow_ref[at]))
            pair = stack(v)
            for j in reversed(range(k)):
                block = (d, slice(k * TILE, (k + 1) * TILE), slice(j * TILE, (j + 1) * TILE))
                step = dot(pair, high_ref[block]) + dot(pair, low_ref[block])
                forward[d][j] = forward[d][j] - fold(step)
            c = coupling_ref[d, k * TILE : (k + 1) * TILE]
            total[d] = total[d] - fold(dot(pair, c))
    for s in range(slots):
        acc = jnp.zeros((cases, LANES), F32)
        for d in range(districts):
            tile, g = s // per, s % per
            within = ids_ref[d, s] % per
            piece = pltpu.roll(
                total[d][:, tile * LANES : (tile + 1) * LANES],
                ((within + per - g) % per) * BS,
                1,
            )
            acc = acc + jnp.where((group == within) & (s < live_ref[d]), piece, 0.0)
        out_ref[s] = acc


def apply(ids, live, gathered, coupling, boundary, prepared):
    scalar = pl.BlockSpec(memory_space=pltpu.SMEM)
    whole = pl.BlockSpec(memory_space=pltpu.VMEM)
    return pl.pallas_call(
        apply_kernel,
        out_shape=jax.ShapeDtypeStruct(gathered.shape, F32),
        in_specs=[scalar, scalar] + [whole] * 7,
        out_specs=whole,
        compiler_params=pltpu.CompilerParams(vmem_limit_bytes=8 << 20),
        cost_estimate=pl.CostEstimate(
            flops=10 * 10**9, bytes_accessed=24 << 20, transcendentals=0
        ),
        name="apply",
    )(ids, live, gathered, coupling, boundary, *prepared)


def body(factor, coupling, boundary, loads, block_ids, live_counts):
    cols = lax.axis_size("col")
    send = jnp.broadcast_to(loads[None], (cols,) + loads.shape)
    gathered = lax.all_to_all(send, "col", 0, 0)
    prepared = prepare(factor)
    back = apply(block_ids, live_counts, gathered, coupling, boundary, prepared)
    return jnp.sum(lax.all_to_all(back, "col", 0, 0), axis=0)


def solution(mesh):
    placed = (
        P(("row", "col"), None, None),
        P(("row", "col"), None, None),
        P(("row", "col"), None, None),
        P(None, ("row", "col")),
        P(("row", "col"), None),
        P(("row", "col")),
    )
    return jax.shard_map(
        body, mesh=mesh, in_specs=placed, out_specs=P(None, ("row", "col")), check_vma=False
    )
```

time: 557 us -> 69.1 us (0.12)
  other arithmetic: 264 us -> 0.63 us
  matrix products: 77.2 us -> 0 us
  local copies, waits for them, and re-layouts: 100 us -> 22.9 us
  waiting for transfers between devices: 71.6 us -> 0.01 us
  Pallas kernels: 0 us -> 21.4 us
  between operations: 14.2 us -> 0.09 us
  blocking collectives: 25.4 us -> 15.7 us
  starting transfers between devices: 0.01 us -> 7.96 us
    another operation x4 -> x0, other arithmetic: 254 us -> none  [district_image(): jax.scipy.linalg.solve_triangular(factor, coupling.astype(jnp.float32), l...]
    another operation x75 -> x0, local copies, waits for them, and re-layouts: 84.9 us -> none  [district_image(): jax.scipy.linalg.solve_triangular(factor, coupling.astype(jnp.float32), l...]
    reduce_scatter x1 -> x0, waiting for transfers between devices: 71.6 us -> none  [body(): return lax.psum_scatter(dense_term, 'col', scatter_dimension=1, tiled=True)]
    another operation x46 -> x0, matrix products: 60 us -> none  [district_image(): jax.scipy.linalg.solve_triangular(factor, coupling.astype(jnp.float32), l...]
    all_gather x1 -> x0, blocking collectives: 25.4 us -> none  [body(): gathered = lax.all_gather(loads, 'col', axis=1, tiled=True)]
    pallas_call x0 -> x2, Pallas kernels: none -> 21.4 us  [the longest x1 11.3 us: prepare(): pl.pallas_call(prepare_kernel, out_shape=(halves, halves, blocks, blocks)...]
    unnamed x18 -> x24, local copies, waits for them, and re-layouts: 0.04 us -> 21.4 us
    dot_general x4 -> x0, matrix products: 16.7 us -> none  [the longest x2 11.8 us: district_image(): lax.dot_general(solved, solved, (((0,), (0,)), ((), ())), precision=lax.P...]
  transfers between devices with their start and end apart: 1 -> 1, of which waited for: 1 -> 0; matrix products, arithmetic and copies ran while one was open for 0% -> 0% of each run, Pallas kernels for 0% -> 16%
where the time goes in v1:
time: 69.1 us; the launch traced here: 68.6 us
  local copies, waits for them, and re-layouts  22.9 us (33%)
  Pallas kernels  21.4 us (31%)
  blocking collectives  15.7 us (23%)
  starting transfers between devices  7.96 us (12%)
    unnamed x24, local copies, waits for them, and re-layouts  21.4 us
    all_to_all x1, blocking collectives, body(): return jnp.sum(lax.all_to_all(back, 'col', 0, 0), axis=0)  15.7 us
    pallas_call x1, Pallas kernels, prepare(): pl.pallas_call(prepare_kernel, out_shape=(halves, halves, blocks, blocks)...  11.3 us
    pallas_call x1, Pallas kernels, apply(): pl.pallas_call(apply_kernel, out_shape=jax.ShapeDtypeStruct(gathered.shap...  10.1 us
    all_to_all x1, starting transfers between devices, body(): gathered = lax.all_to_all(send, 'col', 0, 0)  7.96 us
    broadcast_in_dim x1, local copies, waits for them, and re-layouts, body(): send = jnp.broadcast_to(loads[None], (cols,) + loads.shape)  1.46 us
  transfers between devices with their start and end apart: 1, of which 0 were waited for; matrix products, arithmetic and copies ran while one was open for 0% of the time, Pallas kernels for 16%

profile of v1, /device:TPU:0, one launch (start us, length us, event | category | flops | bytes accessed | tf_op | source)
XLA Modules:
  0.0 68.6 jit_solution(9126575346226642660)
XLA Ops:
  0.0 1.5 %broadcast_in_dim.2 = f32[16,32,128]{2,1,0:T(8,128)} broadcast(f32[32,128]{1,0:T(8,128)} %param.9), dimensions={1,2} | broadcast | bytes 278528 | tf_op jit(solution)/shard_map/broadcast_in_dim | solution.py:248
  1.5 8.0 %all-to-all-start = ((f32[16,32,128]{2,1,0:T(8,128)}), f32[16,32,128]{2,1,0:T(8,128)S(1)}, u32[]{:S(2)}, u32[]{:S(2)}) async-start(f32[16,32,128]{2,1,0:T(8,128)} %broadcast_in_dim.2), calls=%async_computation | async-start | bytes 524288 | tf_op jit(solution)/shard_map/all_to_all | solution.py:249
  9.4 0.0 copy-start
  9.4 0.0 copy-start.2
  9.5 0.0 copy-start.3
  9.5 11.3 %prepare.1 = (bf16[2,1536,1536]{2,1,0:T(8,128)(2,1)S(1)}, bf16[2,1536,1536]{2,1,0:T(8,128)(2,1)S(1)}, bf16[12,256,256]{2,1,0:T(8,128)(2,1)S(1)}, bf16[12,256,256]{2,1,0:T(8,128)(2,1)S(1)}) custom-call(f32[2,1536,1536]{2,1,0:T(8,128)} %factor_ref.1), custom_call_target="tpu_custom_call" | custom-call | flops 20000000000 | bytes 12582912 | tf_op jit(solution)/shard_map/prepare/pallas_call | solution.py:133
  20.8 0.0 copy-start.4
  20.8 3.6 %copy-done.4 = bf16[2,1536,1536]{2,1,0:T(8,128)(2,1)} copy-done((bf16[2,1536,1536]{2,1,0:T(8,128)(2,1)}, bf16[2,1536,1536]{2,1,0:T(8,128)(2,1)S(1)}, u32[]{:S(2)}) %copy-start.4) | copy-done | bytes 9437208
  24.4 3.6 %copy-done.6 = bf16[2,1536,1536]{2,1,0:T(8,128)(2,1)} copy-done((bf16[2,1536,1536]{2,1,0:T(8,128)(2,1)}, bf16[2,1536,1536]{2,1,0:T(8,128)(2,1)S(1)}, u32[]{:S(2)}) %copy-start.6) | copy-done | bytes 9437208
  28.1 1.2 %copy-done.8 = bf16[12,256,256]{2,1,0:T(8,128)(2,1)} copy-done((bf16[12,256,256]{2,1,0:T(8,128)(2,1)}, bf16[12,256,256]{2,1,0:T(8,128)(2,1)S(1)}, u32[]{:S(2)}) %copy-start.8) | copy-done | bytes 1572888
  29.3 1.2 %copy-done.10 = bf16[12,256,256]{2,1,0:T(8,128)(2,1)} copy-done((bf16[12,256,256]{2,1,0:T(8,128)(2,1)}, bf16[12,256,256]{2,1,0:T(8,128)(2,1)S(1)}, u32[]{:S(2)}) %copy-start.10) | copy-done | bytes 1572888
  30.4 0.0 all-to-all-done.gathered_ref
  30.4 0.0 copy-done
  30.4 0.0 copy-done.2
  30.4 0.0 copy-done.3
  30.4 0.0 copy-start.1
  30.4 1.6 %copy-done.1 = f32[2,512,512]{2,1,0:T(8,128)S(1)} copy-done((f32[2,512,512]{2,1,0:T(8,128)S(1)}, f32[2,512,512]{2,1,0:T(8,128)}, u32[]{:S(2)}) %copy-start.1) | copy-done | bytes 2097176
  32.0 3.7 %copy-done.5 = bf16[2,1536,1536]{2,1,0:T(8,128)(2,1)S(1)} copy-done((bf16[2,1536,1536]{2,1,0:T(8,128)(2,1)S(1)}, bf16[2,1536,1536]{2,1,0:T(8,128)(2,1)}, u32[]{:S(2)}) %copy-start.5) | copy-done | bytes 9437208
  35.7 3.7 %copy-done.7 = bf16[2,1536,1536]{2,1,0:T(8,128)(2,1)S(1)} copy-done((bf16[2,1536,1536]{2,1,0:T(8,128)(2,1)S(1)}, bf16[2,1536,1536]{2,1,0:T(8,128)(2,1)}, u32[]{:S(2)}) %copy-start.7) | copy-done | bytes 9437208
  39.4 1.4 %copy-done.9 = bf16[12,256,256]{2,1,0:T(8,128)(2,1)S(1)} copy-done((bf16[12,256,256]{2,1,0:T(8,128)(2,1)S(1)}, bf16[12,256,256]{2,1,0:T(8,128)(2,1)}, u32[]{:S(2)}) %copy-start.9) | copy-done | bytes 1572888
  40.8 1.4 %copy-done.11 = bf16[12,256,256]{2,1,0:T(8,128)(2,1)S(1)} copy-done((bf16[12,256,256]{2,1,0:T(8,128)(2,1)S(1)}, bf16[12,256,256]{2,1,0:T(8,128)(2,1)}, u32[]{:S(2)}) %copy-start.11) | copy-done | bytes 1572888
  42.2 10.1 %apply.1 = f32[16,32,128]{2,1,0:T(8,128)S(1)} custom-call(s32[2,16]{1,0:T(2,128)S(1)} %copy-done.2, s32[2]{0:T(128)S(1)} %copy-done.3, f32[16,32,128]{2,1,0:T(8,128)S(1)} %all-to-all-done.gathered_ref, bf16[2,1536,512]{2,1,0:T(8,128)(2,1)S(1)} %copy-done, f32[2,512,512]{2,1,0:T(8,128)S(1)} %copy-done.1, bf16[2,1536,1536]{2,1,0:T(8,128)(2,1)S(1)} %copy-done.5, ...), custom_call_target="tpu_custom_call" | custom-call | flops 10000000000 | bytes 25165824 | tf_op jit(solution)/shard_map/apply/pallas_call | solution.py:233
  52.3 15.7 %all_to_all.10 = f32[16,32,128]{2,1,0:T(8,128)S(1)} all-to-all(f32[16,32,128]{2,1,0:T(8,128)S(1)} %apply.1), channel_id=1, replica_groups=mesh['row'=8,'col'=16] {'col'}, dimensions={0} | all-to-all | bytes 524288 | tf_op jit(solution)/shard_map/all_to_all | solution.py:252
  68.0 0.6 reduce_sum.9
  (7 shorter events, 0.0 us)
Async XLA Ops:
  1.5 29.0 %all-to-all-start = ((f32[16,32,128]{2,1,0:T(8,128)}), f32[16,32,128]{2,1,0:T(8,128)S(1)}, u32[]{:S(2)}, u32[]{:S(2)}) async-start(f32[16,32,128]{2,1,0:T(8,128)} %broadcast_in_dim.2), calls=%async_computation | async-start | bytes 524288 | tf_op jit(solution)/shard_map/all_to_all | solution.py:249
  9.4 21.0 %copy-start = (bf16[2,1536,512]{2,1,0:T(8,128)(2,1)S(1)}, bf16[2,1536,512]{2,1,0:T(8,128)(2,1)}, u32[]{:S(2)}) copy-start(bf16[2,1536,512]{2,1,0:T(8,128)(2,1)} %coupling_ref.1) | copy-start | bytes 9437188
  9.4 21.0 %copy-start.2 = (s32[2,16]{1,0:T(2,128)S(1)}, s32[2,16]{1,0:T(2,128)}, u32[]{:S(2)}) copy-start(s32[2,16]{1,0:T(2,128)} %ids_ref.1) | copy-start | bytes 388
  9.5 21.0 %copy-start.3 = (s32[2]{0:T(128)S(1)}, s32[2]{0:T(128)}, u32[]{:S(2)}) copy-start(s32[2]{0:T(128)} %live_ref.1) | copy-start | bytes 28
  20.8 3.7 %copy-start.4 = (bf16[2,1536,1536]{2,1,0:T(8,128)(2,1)}, bf16[2,1536,1536]{2,1,0:T(8,128)(2,1)S(1)}, u32[]{:S(2)}) copy-start(bf16[2,1536,1536]{2,1,0:T(8,128)(2,1)S(1)} %get-tuple-element.9.high_ref) | copy-start | bytes 28311556
  24.4 3.6 %copy-start.6 = (bf16[2,1536,1536]{2,1,0:T(8,128)(2,1)}, bf16[2,1536,1536]{2,1,0:T(8,128)(2,1)S(1)}, u32[]{:S(2)}) copy-start(bf16[2,1536,1536]{2,1,0:T(8,128)(2,1)S(1)} %get-tuple-element.10.low_ref) | copy-start | bytes 28311556
  28.1 1.2 %copy-start.8 = (bf16[12,256,256]{2,1,0:T(8,128)(2,1)}, bf16[12,256,256]{2,1,0:T(8,128)(2,1)S(1)}, u32[]{:S(2)}) copy-start(bf16[12,256,256]{2,1,0:T(8,128)(2,1)S(1)} %get-tuple-element.11.ihigh_ref) | copy-start | bytes 4718596
  29.3 1.2 %copy-start.10 = (bf16[12,256,256]{2,1,0:T(8,128)(2,1)}, bf16[12,256,256]{2,1,0:T(8,128)(2,1)S(1)}, u32[]{:S(2)}) copy-start(bf16[12,256,256]{2,1,0:T(8,128)(2,1)S(1)} %get-tuple-element.12.ilow_ref) | copy-start | bytes 4718596
  30.4 1.6 %copy-start.1 = (f32[2,512,512]{2,1,0:T(8,128)S(1)}, f32[2,512,512]{2,1,0:T(8,128)}, u32[]{:S(2)}) copy-start(f32[2,512,512]{2,1,0:T(8,128)} %boundary_ref.1) | copy-start | bytes 6291460
  32.0 3.7 %copy-start.5 = (bf16[2,1536,1536]{2,1,0:T(8,128)(2,1)S(1)}, bf16[2,1536,1536]{2,1,0:T(8,128)(2,1)}, u32[]{:S(2)}) copy-start(bf16[2,1536,1536]{2,1,0:T(8,128)(2,1)} %copy-done.4) | copy-start | bytes 28311556
  35.7 3.7 %copy-start.7 = (bf16[2,1536,1536]{2,1,0:T(8,128)(2,1)S(1)}, bf16[2,1536,1536]{2,1,0:T(8,128)(2,1)}, u32[]{:S(2)}) copy-start(bf16[2,1536,1536]{2,1,0:T(8,128)(2,1)} %copy-done.6) | copy-start | bytes 28311556
  39.4 1.4 %copy-start.9 = (bf16[12,256,256]{2,1,0:T(8,128)(2,1)S(1)}, bf16[12,256,256]{2,1,0:T(8,128)(2,1)}, u32[]{:S(2)}) copy-start(bf16[12,256,256]{2,1,0:T(8,128)(2,1)} %copy-done.8) | copy-start | bytes 4718596
  40.8 1.4 %copy-start.11 = (bf16[12,256,256]{2,1,0:T(8,128)(2,1)S(1)}, bf16[12,256,256]{2,1,0:T(8,128)(2,1)}, u32[]{:S(2)}) copy-start(bf16[12,256,256]{2,1,0:T(8,128)(2,1)} %copy-done.10) | copy-start | bytes 4718596

commit v2 on v1

v2 whole, which is shorter than its diff:
```python
import jax
import jax.numpy as jnp
from jax import lax
from jax.experimental import pallas as pl
from jax.experimental.pallas import tpu as pltpu
from jax.sharding import PartitionSpec as P

BS = 32
TILE = 256
HALF = TILE // 2
BASE = 16
BATCH = 8
LANES = 128
BF = jnp.bfloat16
F32 = jnp.float32


def split(a):
    high = a.astype(BF)
    return high, (a - high.astype(F32)).astype(BF)


def dot(a, b):
    return jnp.dot(a, b, preferred_element_type=F32)


def dot_t(a, b):
    return lax.dot_general(a, b, (((1,), (1,)), ((), ())), preferred_element_type=F32)


def dot3(a, b):
    both = dot(jnp.concatenate([a[0], a[1]], axis=1), jnp.concatenate([b[0], b[0]], axis=0))
    return both + dot(a[0], b[1])


def base_inverses(tiles):
    lane = lax.broadcasted_iota(jnp.int32, (BASE, LANES), 1)
    row = lax.broadcasted_iota(jnp.int32, (BASE, LANES), 0)
    group, column = lane // BASE, lane % BASE
    units, recips, states = [], [], []
    for tile in tiles:
        packed = tile[:BASE]
        for b in range(1, LANES // BASE):
            packed = jnp.where(group == b, tile[b * BASE : (b + 1) * BASE], packed)
        diagonal = jnp.sum(jnp.where(row == column, packed, 0.0), axis=0, keepdims=True)
        recip = 1.0 / diagonal
        recips.append(recip)
        units.append(jnp.where(row > column, packed * recip, 0.0))
        acc = jnp.where(row == column, 1.0, 0.0).astype(F32)
        states.append([acc[8 * g : 8 * g + 8] for g in range(BASE // 8)])
    for j in range(BASE - 1):
        index = group[:8] * BASE + j
        for unit, parts in zip(units, states):
            pivot = parts[j // 8][j % 8 : j % 8 + 1]
            for g in range((j + 1) // 8, BASE // 8):
                factor = jnp.take_along_axis(unit[8 * g : 8 * g + 8], index, axis=1)
                parts[g] = parts[g] - factor * pivot
    results = []
    for recip, parts in zip(recips, states):
        scale = jnp.take_along_axis(
            jnp.broadcast_to(recip, (BASE, LANES)), group * BASE + row, axis=1
        )
        inverse = jnp.concatenate(parts, axis=0) * scale
        results.append(
            jnp.concatenate(
                [jnp.where(group == b, inverse, 0.0) for b in range(LANES // BASE)], axis=0
            )
        )
    return results


def prepare_kernel(factor_ref, inverse_ref, held, inv, inverse, sem, out_sem):
    districts, size, _ = factor_ref.shape
    steps = size // TILE
    blocks = [(d, k) for k in range(steps) for d in range(districts)]
    loads, stores = {}, []
    for d, k in blocks:
        at = (d, pl.ds(k * TILE, TILE), pl.ds(k * TILE, TILE))
        loads[d, k] = pltpu.make_async_copy(
            factor_ref.at[at], held.at[d * steps + k], sem.at[d * steps + k]
        )
        loads[d, k].start()
    row = lax.broadcasted_iota(jnp.int32, (LANES, LANES), 0)
    col = lax.broadcasted_iota(jnp.int32, (LANES, LANES), 1)
    tiles = [(d * steps + k, t) for d, k in blocks for t in range(2)]

    def tile_at(at, t, u):
        return held[at, pl.ds(t * HALF, HALF), pl.ds(u * HALF, HALF)]

    for first in range(0, len(tiles), BATCH):
        batch = tiles[first : first + BATCH]
        for at, t in batch:
            if t == 0:
                loads[at // steps, at % steps].wait()
        for (at, t), x in zip(batch, base_inverses([tile_at(at, t, t) for at, t in batch])):
            inv[2 * at + t] = x
    width = BASE
    while width < HALF:
        mask = (
            (row // (2 * width) == col // (2 * width))
            & (row % (2 * width) >= width)
            & (col % (2 * width) < width)
        )
        for at, t in tiles:
            x = inv[2 * at + t]
            pair = split(x)
            off = split(jnp.where(mask, tile_at(at, t, t), 0.0))
            inv[2 * at + t] = x - dot3(pair, split(dot3(off, pair)))
        width *= 2
    for d, k in blocks:
        at = d * steps + k
        top, bottom = split(inv[2 * at]), split(inv[2 * at + 1])
        off = split(tile_at(at, 1, 0))
        left = split(-dot3(bottom, split(dot3(off, top))))
        zero = jnp.zeros((HALF, HALF), BF)
        for i in range(2):
            inverse[at, i, :HALF, :HALF] = top[i]
            inverse[at, i, :HALF, HALF:] = zero
            inverse[at, i, HALF:, :HALF] = left[i]
            inverse[at, i, HALF:, HALF:] = bottom[i]
        stores.append(pltpu.make_async_copy(inverse.at[at], inverse_ref.at[at], out_sem.at[at]))
        stores[-1].start()
    for copy in stores:
        copy.wait()


def prepare(factor):
    districts, size, _ = factor.shape
    count = districts * (size // TILE)
    blocks = (count, 2, TILE, TILE)
    anywhere = pl.BlockSpec(memory_space=pltpu.HBM)
    return pl.pallas_call(
        prepare_kernel,
        out_shape=jax.ShapeDtypeStruct(blocks, BF),
        in_specs=[anywhere],
        out_specs=anywhere,
        scratch_shapes=[
            pltpu.VMEM((count, TILE, TILE), F32),
            pltpu.VMEM((count * 2, LANES, LANES), F32),
            pltpu.VMEM(blocks, BF),
            pltpu.SemaphoreType.DMA((count,)),
            pltpu.SemaphoreType.DMA((count,)),
        ],
        compiler_params=pltpu.CompilerParams(vmem_limit_bytes=61 << 20),
        cost_estimate=pl.CostEstimate(
            flops=20 * 10**9, bytes_accessed=12 << 20, transcendentals=0
        ),
        name="prepare",
    )(factor)


def apply_kernel(
    ids_ref,
    live_ref,
    gathered_ref,
    coupling_ref,
    factor_ref,
    boundary_ref,
    inverse_ref,
    out_ref,
    held,
    high,
    low,
    coupling,
    inverse,
    sem,
    inv_sem,
    cpl_sem,
):
    slots, cases, _ = gathered_ref.shape
    districts, size, faces = coupling_ref.shape
    steps = size // TILE
    per = LANES // BS
    group = lax.broadcasted_iota(jnp.int32, (cases, LANES), 1) // BS

    def start(src, dst, at, semaphore):
        copy = pltpu.make_async_copy(src.at[at], dst.at[at], semaphore)
        copy.start()
        return copy

    couplings, inverses, panels = {}, {}, {}
    for d in range(districts):
        couplings[d] = start(coupling_ref, coupling, d, cpl_sem.at[d])
    for k in range(steps):
        for d in range(districts):
            at = d * steps + k
            inverses[d, k] = start(inverse_ref, inverse, at, inv_sem.at[at])
            if k < steps - 1:
                at = (d, pl.ds((k + 1) * TILE, size - (k + 1) * TILE), pl.ds(k * TILE, TILE))
                panels[d, k] = start(factor_ref, held, at, sem.at[d, k])
    def stack(a):
        return jnp.concatenate(split(a), axis=0)

    def fold(a):
        return a[:cases] + a[cases:]

    masked, total, rest = [], [], []
    for d in range(districts):
        columns = []
        for tile in range(slots // per):
            acc = jnp.zeros((cases, LANES), F32)
            for g in range(per):
                s = tile * per + g
                within = ids_ref[d, s] % per
                piece = pltpu.roll(gathered_ref[s], ((g + per - within) % per) * BS, 1)
                acc = jnp.where((group == g) & (s < live_ref[d]), piece, acc)
            columns.append(acc)
        x = stack(jnp.concatenate(columns, axis=1))
        parts = split(boundary_ref[d])
        total.append(fold(dot_t(x, parts[0]) + dot_t(x, parts[1])))
        masked.append(x)
    for d in range(districts):
        couplings[d].wait()
    for d in range(districts):
        right = dot_t(masked[d], coupling[d])
        rest.append([fold(right[:, k * TILE : (k + 1) * TILE]) for k in range(steps)])
    forward = [[None] * steps for _ in range(districts)]
    for k in range(steps):
        if k < 3:
            for copies in (inverses, panels):
                for (d, at), copy in copies.items():
                    if min(at, 2) == k:
                        copy.wait()
        for d in range(districts):
            r = stack(rest[d][k])
            at = d * steps + k
            u = fold(dot_t(r, inverse[at, 0]) + dot_t(r, inverse[at, 1]))
            forward[d][k] = u
            pair = stack(u)
            for j in range(k + 1, steps):
                block = (d, slice(j * TILE, (j + 1) * TILE), slice(k * TILE, (k + 1) * TILE))
                parts = split(held[block])
                high[block], low[block] = parts
                step = dot_t(pair, parts[0]) + dot_t(pair, parts[1])
                rest[d][j] = rest[d][j] - fold(step)
    for k in reversed(range(steps)):
        for d in range(districts):
            r = stack(forward[d][k])
            at = d * steps + k
            v = fold(dot(r, inverse[at, 0]) + dot(r, inverse[at, 1]))
            pair = stack(v)
            for j in reversed(range(k)):
                block = (d, slice(k * TILE, (k + 1) * TILE), slice(j * TILE, (j + 1) * TILE))
                step = dot(pair, high[block]) + dot(pair, low[block])
                forward[d][j] = forward[d][j] - fold(step)
            c = coupling[d, k * TILE : (k + 1) * TILE]
            total[d] = total[d] - fold(dot(pair, c))
    for s in range(slots):
        acc = jnp.zeros((cases, LANES), F32)
        for d in range(districts):
            tile, g = s // per, s % per
            within = ids_ref[d, s] % per
            piece = pltpu.roll(
                total[d][:, tile * LANES : (tile + 1) * LANES],
                ((within + per - g) % per) * BS,
                1,
            )
            acc = acc + jnp.where((group == within) & (s < live_ref[d]), piece, 0.0)
        out_ref[s] = acc


def apply(ids, live, gathered, coupling, factor, boundary, inverse):
    districts, size, faces = coupling.shape
    steps = size // TILE
    scalar = pl.BlockSpec(memory_space=pltpu.SMEM)
    whole = pl.BlockSpec(memory_space=pltpu.VMEM)
    anywhere = pl.BlockSpec(memory_space=pltpu.HBM)
    return pl.pallas_call(
        apply_kernel,
        out_shape=jax.ShapeDtypeStruct(gathered.shape, F32),
        in_specs=[scalar, scalar, whole, anywhere, anywhere, whole, anywhere],
        out_specs=whole,
        scratch_shapes=[
            pltpu.VMEM((districts, size, size - TILE), F32),
            pltpu.VMEM((districts, size, size - TILE), BF),
            pltpu.VMEM((districts, size, size - TILE), BF),
            pltpu.VMEM(coupling.shape, BF),
            pltpu.VMEM(inverse.shape, BF),
            pltpu.SemaphoreType.DMA((districts, steps - 1)),
            pltpu.SemaphoreType.DMA((districts * steps,)),
            pltpu.SemaphoreType.DMA((districts,)),
        ],
        compiler_params=pltpu.CompilerParams(vmem_limit_bytes=50 << 20),
        cost_estimate=pl.CostEstimate(
            flops=10 * 10**9, bytes_accessed=24 << 20, transcendentals=0
        ),
        name="apply",
    )(ids, live, gathered, coupling, factor, boundary, inverse)


def body(factor, coupling, boundary, loads, block_ids, live_counts):
    cols = lax.axis_size("col")
    send = jnp.broadcast_to(loads[None], (cols,) + loads.shape)
    gathered = lax.all_to_all(send, "col", 0, 0)
    back = apply(
        block_ids, live_counts, gathered, coupling, factor, boundary, prepare(factor)
    )
    return jnp.sum(lax.all_to_all(back, "col", 0, 0), axis=0)


def solution(mesh):
    placed = (
        P(("row", "col"), None, None),
        P(("row", "col"), None, None),
        P(("row", "col"), None, None),
        P(None, ("row", "col")),
        P(("row", "col"), None),
        P(("row", "col")),
    )
    return jax.shard_map(
        body, mesh=mesh, in_specs=placed, out_specs=P(None, ("row", "col")), check_vma=False
    )
```

time: 69.1 us -> 49.9 us (0.72)
  local copies, waits for them, and re-layouts: 22.9 us -> 1.46 us
  Pallas kernels: 21.4 us -> 23.7 us
    unnamed x24 -> x6, local copies, waits for them, and re-layouts: 21.4 us -> 0.02 us
    pallas_call x1, Pallas kernels: 10.1 us -> 15.6 us  [apply(): pl.pallas_call(apply_kernel, out_shape=jax.ShapeDtypeStruct(gathered.shap...]
    pallas_call x1, Pallas kernels: 11.3 us -> 8.06 us  [prepare(): pl.pallas_call(prepare_kernel, out_shape=jax.ShapeDtypeStruct(blocks, BF)...]
  transfers between devices with their start and end apart: 1 -> 1, of which waited for: 0 -> 1; matrix products, arithmetic and copies ran while one was open for 0% -> 0% of each run, Pallas kernels for 16% -> 16%
where the time goes in v2:
time: 49.9 us; the launch traced here: 49.5 us
  Pallas kernels  23.7 us (47%)
  blocking collectives  15.1 us (30%)
  starting transfers between devices  7.96 us (16%)
  local copies, waits for them, and re-layouts  1.46 us (3%)
  other arithmetic  0.63 us (1%)
  waiting for transfers between devices  0.59 us (1%)
    pallas_call x1, Pallas kernels, apply(): pl.pallas_call(apply_kernel, out_shape=jax.ShapeDtypeStruct(gathered.shap...  15.6 us
    all_to_all x1, blocking collectives, body(): return jnp.sum(lax.all_to_all(back, 'col', 0, 0), axis=0)  15.1 us
    pallas_call x1, Pallas kernels, prepare(): pl.pallas_call(prepare_kernel, out_shape=jax.ShapeDtypeStruct(blocks, BF)...  8.06 us
    all_to_all x1, starting transfers between devices, body(): gathered = lax.all_to_all(send, 'col', 0, 0)  7.96 us
    broadcast_in_dim x1, local copies, waits for them, and re-layouts, body(): send = jnp.broadcast_to(loads[None], (cols,) + loads.shape)  1.44 us
  transfers between devices with their start and end apart: 1, of which 1 were waited for; matrix products, arithmetic and copies ran while one was open for 0% of the time, Pallas kernels for 16%

profile of v2, /device:TPU:0, one launch (start us, length us, event | category | flops | bytes accessed | tf_op | source)
XLA Modules:
  0.0 49.5 jit_solution(10566225636036265546)
XLA Ops:
  0.0 1.4 %broadcast_in_dim.2 = f32[16,32,128]{2,1,0:T(8,128)} broadcast(f32[32,128]{1,0:T(8,128)} %param.9), dimensions={1,2} | broadcast | bytes 278528 | tf_op jit(solution)/shard_map/broadcast_in_dim | solution.py:293
  1.4 8.0 %all-to-all-start = ((f32[16,32,128]{2,1,0:T(8,128)}), f32[16,32,128]{2,1,0:T(8,128)S(1)}, u32[]{:S(2)}, u32[]{:S(2)}) async-start(f32[16,32,128]{2,1,0:T(8,128)} %broadcast_in_dim.2), calls=%async_computation | async-start | bytes 524288 | tf_op jit(solution)/shard_map/all_to_all | solution.py:294
  9.4 0.0 copy-start
  9.4 0.0 copy-start.1
  9.4 0.0 copy-start.2
  9.4 8.1 %prepare.1.inverse_ref = bf16[12,2,256,256]{3,2,1,0:T(8,128)(2,1)} custom-call(f32[2,1536,1536]{2,1,0:T(8,128)} %factor_ref.3), custom_call_target="tpu_custom_call" | custom-call | flops 20000000000 | bytes 12582912 | tf_op jit(solution)/shard_map/prepare/pallas_call | solution.py:132
  17.5 0.6 %all-to-all-done.gathered_ref = f32[16,32,128]{2,1,0:T(8,128)S(1)} async-done(((f32[16,32,128]{2,1,0:T(8,128)}), f32[16,32,128]{2,1,0:T(8,128)S(1)}, u32[]{:S(2)}, u32[]{:S(2)}) %all-to-all-start) | async-done | bytes 262176 | tf_op jit(solution)/shard_map/all_to_all | solution.py:294
  18.1 0.0 copy-done
  18.1 0.0 copy-done.1
  18.1 0.0 copy-done.2
  18.1 15.6 %apply.1 = f32[16,32,128]{2,1,0:T(8,128)S(1)} custom-call(s32[2,16]{1,0:T(2,128)S(1)} %copy-done.1, s32[2]{0:T(128)S(1)} %copy-done.2, f32[16,32,128]{2,1,0:T(8,128)S(1)} %all-to-all-done.gathered_ref, bf16[2,1536,512]{2,1,0:T(8,128)(2,1)} %coupling_ref.1, f32[2,1536,1536]{2,1,0:T(8,128)} %factor_ref.3, f32[2,512,512]{2,1,0:T(8,128)S(1)} %copy-done, ...), custom_call_target="tpu_custom_call" | custom-call | flops 10000000000 | bytes 25165824 | tf_op jit(solution)/shard_map/apply/pallas_call | solution.py:268
  33.8 15.1 %all_to_all.10 = f32[16,32,128]{2,1,0:T(8,128)S(1)} all-to-all(f32[16,32,128]{2,1,0:T(8,128)S(1)} %apply.1), channel_id=1, replica_groups=mesh['row'=8,'col'=16] {'col'}, dimensions={0} | all-to-all | bytes 524288 | tf_op jit(solution)/shard_map/all_to_all | solution.py:298
  48.9 0.6 %reduce_sum.9 = f32[32,128]{1,0:T(8,128)} reduce(f32[16,32,128]{2,1,0:T(8,128)S(1)} %all_to_all.10, f32[]{:T(128)} %constant.0.clone.1), dimensions={0}, to_apply=%region_0.0 | reduce | flops 61440 | bytes 278532 | tf_op jit(solution)/shard_map/reduce_sum | solution.py:298
Async XLA Ops:
  1.4 16.7 %all-to-all-start = ((f32[16,32,128]{2,1,0:T(8,128)}), f32[16,32,128]{2,1,0:T(8,128)S(1)}, u32[]{:S(2)}, u32[]{:S(2)}) async-start(f32[16,32,128]{2,1,0:T(8,128)} %broadcast_in_dim.2), calls=%async_computation | async-start | bytes 524288 | tf_op jit(solution)/shard_map/all_to_all | solution.py:294
  9.4 8.7 %copy-start = (f32[2,512,512]{2,1,0:T(8,128)S(1)}, f32[2,512,512]{2,1,0:T(8,128)}, u32[]{:S(2)}) copy-start(f32[2,512,512]{2,1,0:T(8,128)} %boundary_ref.1) | copy-start | bytes 6291460
  9.4 8.7 %copy-start.1 = (s32[2,16]{1,0:T(2,128)S(1)}, s32[2,16]{1,0:T(2,128)}, u32[]{:S(2)}) copy-start(s32[2,16]{1,0:T(2,128)} %ids_ref.1) | copy-start | bytes 388
  9.4 8.7 %copy-start.2 = (s32[2]{0:T(128)S(1)}, s32[2]{0:T(128)}, u32[]{:S(2)}) copy-start(s32[2]{0:T(128)} %live_ref.1) | copy-start | bytes 28

commit v3 on v2

--- a/solution.py
+++ b/solution.py
@@ -9,7 +9,7 @@
 TILE = 256
 HALF = TILE // 2
 BASE = 16
-BATCH = 8
+BATCH = 12
 LANES = 128
 BF = jnp.bfloat16
 F32 = jnp.float32
@@ -60,11 +60,39 @@
         scale = jnp.take_along_axis(
             jnp.broadcast_to(recip, (BASE, LANES)), group * BASE + row, axis=1
         )
-        inverse = jnp.concatenate(parts, axis=0) * scale
+        results.append(jnp.concatenate(parts, axis=0) * scale)
+    return results
+
+
+def doubled(tiles, packed, width):
+    group = lax.broadcasted_iota(jnp.int32, (width, LANES), 1) // width
+    even = group % 2 == 0
+    count = LANES // width
+    products = []
+    for tile, x in zip(tiles, packed):
+        below = jnp.where(group == 0, tile[width : 2 * width], 0.0)
+        for b in range(2, count, 2):
+            below = jnp.where(group == b, tile[(b + 1) * width : (b + 2) * width], below)
+        below = jnp.concatenate(split(below), axis=0)
+        spread = [
+            jnp.where(group == b, half, jnp.zeros_like(half))
+            for half in split(x)
+            for b in range(count)
+        ]
+        product = dot(jnp.concatenate([below, below], axis=1), jnp.concatenate(spread, axis=0))
+        products.append(product[:width] + product[width:])
+    results = []
+    for x, product in zip(packed, products):
+        odd = jnp.concatenate(split(jnp.where(even, 0.0, x)), axis=0)
+        spread = []
+        for half in split(product):
+            zero = jnp.zeros_like(half)
+            for b in range(0, count, 2):
+                spread += [zero, jnp.where(group == b, half, zero)]
+        product = dot(jnp.concatenate([odd, odd], axis=1), jnp.concatenate(spread, axis=0))
+        corner = product[:width] + product[width:]
         results.append(
-            jnp.concatenate(
-                [jnp.where(group == b, inverse, 0.0) for b in range(LANES // BASE)], axis=0
-            )
+            jnp.concatenate([jnp.where(even, x, 0.0), jnp.where(even, -corner, x)], axis=0)
         )
     return results
 
@@ -80,8 +108,6 @@
             factor_ref.at[at], held.at[d * steps + k], sem.at[d * steps + k]
         )
         loads[d, k].start()
-    row = lax.broadcasted_iota(jnp.int32, (LANES, LANES), 0)
-    col = lax.broadcasted_iota(jnp.int32, (LANES, LANES), 1)
     tiles = [(d * steps + k, t) for d, k in blocks for t in range(2)]
 
     def tile_at(at, t, u):
@@ -92,34 +118,30 @@
         for at, t in batch:
             if t == 0:
                 loads[at // steps, at % steps].wait()
-        for (at, t), x in zip(batch, base_inverses([tile_at(at, t, t) for at, t in batch])):
+        diagonal = [tile_at(at, t, t) for at, t in batch]
+        packed = base_inverses(diagonal)
+        width = BASE
+        while width < HALF:
+            packed = doubled(diagonal, packed, width)
+            width *= 2
+        for (at, t), x in zip(batch, packed):
             inv[2 * at + t] = x
-    width = BASE
-    while width < HALF:
-        mask = (
-            (row // (2 * width) == col // (2 * width))
-            & (row % (2 * width) >= width)
-            & (col % (2 * width) < width)
-        )
-        for at, t in tiles:
-            x = inv[2 * at + t]
-            pair = split(x)
-            off = split(jnp.where(mask, tile_at(at, t, t), 0.0))
-            inv[2 * at + t] = x - dot3(pair, split(dot3(off, pair)))
-        width *= 2
-    for d, k in blocks:
-        at = d * steps + k
-        top, bottom = split(inv[2 * at]), split(inv[2 * at + 1])
-        off = split(tile_at(at, 1, 0))
-        left = split(-dot3(bottom, split(dot3(off, top))))
+    for first in range(0, len(blocks), BATCH // 2):
+        group = [d * steps + k for d, k in blocks[first : first + BATCH // 2]]
+        pairs = [(split(inv[2 * at]), split(inv[2 * at + 1])) for at in group]
+        lefts = [dot3(split(tile_at(at, 1, 0)), top) for at, (top, _) in zip(group, pairs)]
+        lefts = [split(-dot3(bottom, split(x))) for x, (_, bottom) in zip(lefts, pairs)]
         zero = jnp.zeros((HALF, HALF), BF)
-        for i in range(2):
-            inverse[at, i, :HALF, :HALF] = top[i]
-            inverse[at, i, :HALF, HALF:] = zero
-            inverse[at, i, HALF:, :HALF] = left[i]
-            inverse[at, i, HALF:, HALF:] = bottom[i]
-        stores.append(pltpu.make_async_copy(inverse.at[at], inverse_ref.at[at], out_sem.at[at]))
-        stores[-1].start()
+        for at, (top, bottom), left in zip(group, pairs, lefts):
+            for i in range(2):
+                inverse[at, i, :HALF, :HALF] = top[i]
+                inverse[at, i, :HALF, HALF:] = zero
+                inverse[at, i, HALF:, :HALF] = left[i]
+                inverse[at, i, HALF:, HALF:] = bottom[i]
+            stores.append(
+                pltpu.make_async_copy(inverse.at[at], inverse_ref.at[at], out_sem.at[at])
+            )
+            stores[-1].start()
     for copy in stores:
         copy.wait()
 
@@ -173,21 +195,37 @@
     per = LANES // BS
     group = lax.broadcasted_iota(jnp.int32, (cases, LANES), 1) // BS
 
-    def start(src, dst, at, semaphore):
-        copy = pltpu.make_async_copy(src.at[at], dst.at[at], semaphore)
-        copy.start()
-        return copy
-
-    couplings, inverses, panels = {}, {}, {}
-    for d in range(districts):
-        couplings[d] = start(coupling_ref, coupling, d, cpl_sem.at[d])
+    couplings = [
+        pltpu.make_async_copy(coupling_ref.at[d], coupling.at[d], cpl_sem.at[d])
+        for d in range(districts)
+    ]
+    stages = []
     for k in range(steps):
+        copies = []
         for d in range(districts):
             at = d * steps + k
-            inverses[d, k] = start(inverse_ref, inverse, at, inv_sem.at[at])
+            copies.append(
+                pltpu.make_async_copy(inverse_ref.at[at], inverse.at[at], inv_sem.at[at])
+            )
             if k < steps - 1:
                 at = (d, pl.ds((k + 1) * TILE, size - (k + 1) * TILE), pl.ds(k * TILE, TILE))
-                panels[d, k] = start(factor_ref, held, at, sem.at[d, k])
+                copies.append(
+                    pltpu.make_async_copy(factor_ref.at[at], held.at[at], sem.at[d, k])
+                )
+        stages.append(copies)
+    stages[2] = sum(stages[2:], [])
+
+    def start(copies):
+        for copy in copies:
+            copy.start()
+
+    def wait(copies):
+        for copy in copies:
+            copy.wait()
+
+    start(couplings)
+    start(stages[0])
+
     def stack(a):
         return jnp.concatenate(split(a), axis=0)
 
@@ -206,45 +244,74 @@
                 acc = jnp.where((group == g) & (s < live_ref[d]), piece, acc)
             columns.append(acc)
         x = stack(jnp.concatenate(columns, axis=1))
+        masked.append(x)
+    start(stages[1])
+    for d in range(districts):
         parts = split(boundary_ref[d])
-        total.append(fold(dot_t(x, parts[0]) + dot_t(x, parts[1])))
-        masked.append(x)
+        total.append(fold(dot_t(masked[d], parts[0]) + dot_t(masked[d], parts[1])))
     for d in range(districts):
-        couplings[d].wait()
-    for d in range(districts):
+        wait(couplings[d : d + 1])
+        if d == 0:
+            start(stages[2])
         right = dot_t(masked[d], coupling[d])
         rest.append([fold(right[:, k * TILE : (k + 1) * TILE]) for k in range(steps)])
-    forward = [[None] * steps for _ in range(districts)]
+    everyone = range(districts)
+    forward = [[None] * steps for _ in everyone]
+    pairs = {}
+
+    def advance(d, k):
+        at = d * steps + k
+        r = stack(rest[d][k])
+        forward[d][k] = fold(dot_t(r, inverse[at, 0]) + dot_t(r, inverse[at, 1]))
+        pairs[d, k] = stack(forward[d][k])
+
+    def update(d, k, j):
+        block = (d, slice(j * TILE, (j + 1) * TILE), slice(k * TILE, (k + 1) * TILE))
+        parts = split(held[block])
+        high[block], low[block] = parts
+        step = dot_t(pairs[d, k], parts[0]) + dot_t(pairs[d, k], parts[1])
+        rest[d][j] = rest[d][j] - fold(step)
+
     for k in range(steps):
         if k < 3:
-            for copies in (inverses, panels):
-                for (d, at), copy in copies.items():
-                    if min(at, 2) == k:
-                        copy.wait()
-        for d in range(districts):
-            r = stack(rest[d][k])
-            at = d * steps + k
-            u = fold(dot_t(r, inverse[at, 0]) + dot_t(r, inverse[at, 1]))
-            forward[d][k] = u
-            pair = stack(u)
-            for j in range(k + 1, steps):
-                block = (d, slice(j * TILE, (j + 1) * TILE), slice(k * TILE, (k + 1) * TILE))
-                parts = split(held[block])
-                high[block], low[block] = parts
-                step = dot_t(pair, parts[0]) + dot_t(pair, parts[1])
-                rest[d][j] = rest[d][j] - fold(step)
+            wait(stages[k])
+        for d in everyone:
+            advance(d, k)
+        for d in everyone:
+            if d == 1 and k + 1 < steps:
+                for e in everyone:
+                    update(e, k, k + 1)
+            if k > 0:
+                for j in range(k + 1, steps):
+                    update(d, k - 1, j)
+
+    def retreat(d, k):
+        at = d * steps + k
+        r = stack(forward[d][k])
+        pairs[d, k] = stack(fold(dot(r, inverse[at, 0]) + dot(r, inverse[at, 1])))
+
+    def downdate(d, k, j):
+        block = (d, slice(k * TILE, (k + 1) * TILE), slice(j * TILE, (j + 1) * TILE))
+        step = dot(pairs[d, k], high[block]) + dot(pairs[d, k], low[block])
+        forward[d][j] = forward[d][j] - fold(step)
+
+    def finish(d, k):
+        c = coupling[d, k * TILE : (k + 1) * TILE]
+        total[d] = total[d] - fold(dot(pairs[d, k], c))
+
     for k in reversed(range(steps)):
-        for d in range(districts):
-            r = stack(forward[d][k])
-            at = d * steps + k
-            v = fold(dot(r, inverse[at, 0]) + dot(r, inverse[at, 1]))
-            pair = stack(v)
-            for j in reversed(range(k)):
-                block = (d, slice(k * TILE, (k + 1) * TILE), slice(j * TILE, (j + 1) * TILE))
-                step = dot(pair, high[block]) + dot(pair, low[block])
-                forward[d][j] = forward[d][j] - fold(step)
-            c = coupling[d, k * TILE : (k + 1) * TILE]
-            total[d] = total[d] - fold(dot(pair, c))
+        for d in everyone:
+            retreat(d, k)
+        for d in everyone:
+            if d == 1 and k > 0:
+                for e in everyone:
+                    downdate(e, k, k - 1)
+            if k + 1 < steps:
+                finish(d, k + 1)
+                for j in reversed(range(k)):
+                    downdate(d, k + 1, j)
+    for d in everyone:
+        finish(d, 0)
     for s in range(slots):
         acc = jnp.zeros((cases, LANES), F32)
         for d in range(districts):

time: 49.9 us -> 45 us (0.902)
  Pallas kernels: 23.7 us -> 18.9 us
  waiting for transfers between devices: 0.59 us -> 1.24 us
  blocking collectives: 15.1 us -> 14.5 us
    pallas_call x1, Pallas kernels: 15.6 us -> 11.5 us  [apply(): pl.pallas_call(apply_kernel, out_shape=jax.ShapeDtypeStruct(gathered.shap...]
    all_to_all x1, waiting for transfers between devices: 0.59 us -> 1.24 us  [body(): gathered = lax.all_to_all(send, 'col', 0, 0)]
    pallas_call x1, Pallas kernels: 8.06 us -> 7.41 us  [prepare(): pl.pallas_call(prepare_kernel, out_shape=jax.ShapeDtypeStruct(blocks, BF)...]
    all_to_all x1, blocking collectives: 15.1 us -> 14.5 us  [body(): return jnp.sum(lax.all_to_all(back, 'col', 0, 0), axis=0)]
  transfers between devices with their start and end apart: 1 -> 1, of which waited for: 1 -> 1; matrix products, arithmetic and copies ran while one was open for 0% -> 0% of each run, Pallas kernels for 16% -> 17%
where the time goes in v3:
time: 45 us; the launch traced here: 44.7 us
  Pallas kernels  18.9 us (42%)
  blocking collectives  14.5 us (32%)
  starting transfers between devices  7.96 us (18%)
  local copies, waits for them, and re-layouts  1.46 us (3%)
  waiting for transfers between devices  1.24 us (3%)
  other arithmetic  0.63 us (1%)
    all_to_all x1, blocking collectives, body(): return jnp.sum(lax.all_to_all(back, 'col', 0, 0), axis=0)  14.5 us
    pallas_call x1, Pallas kernels, apply(): pl.pallas_call(apply_kernel, out_shape=jax.ShapeDtypeStruct(gathered.shap...  11.5 us
    all_to_all x1, starting transfers between devices, body(): gathered = lax.all_to_all(send, 'col', 0, 0)  7.96 us
    pallas_call x1, Pallas kernels, prepare(): pl.pallas_call(prepare_kernel, out_shape=jax.ShapeDtypeStruct(blocks, BF)...  7.41 us
    broadcast_in_dim x1, local copies, waits for them, and re-layouts, body(): send = jnp.broadcast_to(loads[None], (cols,) + loads.shape)  1.44 us
    all_to_all x1, waiting for transfers between devices, body(): gathered = lax.all_to_all(send, 'col', 0, 0)  1.24 us
  transfers between devices with their start and end apart: 1, of which 1 were waited for; matrix products, arithmetic and copies ran while one was open for 0% of the time, Pallas kernels for 17%

profile of v3, /device:TPU:0, one launch (start us, length us, event | category | flops | bytes accessed | tf_op | source)
XLA Modules:
  0.0 44.7 jit_solution(7845412572659723822)
XLA Ops:
  0.0 1.4 %broadcast_in_dim.2 = f32[16,32,128]{2,1,0:T(8,128)} broadcast(f32[32,128]{1,0:T(8,128)} %param.9), dimensions={1,2} | broadcast | bytes 278528 | tf_op jit(solution)/shard_map/broadcast_in_dim | solution.py:360
  1.4 8.0 %all-to-all-start = ((f32[16,32,128]{2,1,0:T(8,128)}), f32[16,32,128]{2,1,0:T(8,128)S(1)}, u32[]{:S(2)}, u32[]{:S(2)}) async-start(f32[16,32,128]{2,1,0:T(8,128)} %broadcast_in_dim.2), calls=%async_computation | async-start | bytes 524288 | tf_op jit(solution)/shard_map/all_to_all | solution.py:361
  9.4 0.0 copy-start
  9.4 0.0 copy-start.1
  9.4 0.0 copy-start.2
  9.4 7.4 %prepare.1.inverse_ref = bf16[12,2,256,256]{3,2,1,0:T(8,128)(2,1)} custom-call(f32[2,1536,1536]{2,1,0:T(8,128)} %factor_ref.3), custom_call_target="tpu_custom_call" | custom-call | flops 20000000000 | bytes 12582912 | tf_op jit(solution)/shard_map/prepare/pallas_call | solution.py:154
  16.9 1.2 %all-to-all-done.gathered_ref = f32[16,32,128]{2,1,0:T(8,128)S(1)} async-done(((f32[16,32,128]{2,1,0:T(8,128)}), f32[16,32,128]{2,1,0:T(8,128)S(1)}, u32[]{:S(2)}, u32[]{:S(2)}) %all-to-all-start) | async-done | bytes 262176 | tf_op jit(solution)/shard_map/all_to_all | solution.py:361
  18.1 0.0 copy-done
  18.1 0.0 copy-done.1
  18.1 0.0 copy-done.2
  18.1 11.5 %apply.1 = f32[16,32,128]{2,1,0:T(8,128)S(1)} custom-call(s32[2,16]{1,0:T(2,128)S(1)} %copy-done.1, s32[2]{0:T(128)S(1)} %copy-done.2, f32[16,32,128]{2,1,0:T(8,128)S(1)} %all-to-all-done.gathered_ref, bf16[2,1536,512]{2,1,0:T(8,128)(2,1)} %coupling_ref.1, f32[2,1536,1536]{2,1,0:T(8,128)} %factor_ref.3, f32[2,512,512]{2,1,0:T(8,128)S(1)} %copy-done, ...), custom_call_target="tpu_custom_call" | custom-call | flops 10000000000 | bytes 25165824 | tf_op jit(solution)/shard_map/apply/pallas_call | solution.py:335
  29.6 14.5 %all_to_all.10 = f32[16,32,128]{2,1,0:T(8,128)S(1)} all-to-all(f32[16,32,128]{2,1,0:T(8,128)S(1)} %apply.1), channel_id=1, replica_groups=mesh['row'=8,'col'=16] {'col'}, dimensions={0} | all-to-all | bytes 524288 | tf_op jit(solution)/shard_map/all_to_all | solution.py:365
  44.1 0.6 %reduce_sum.9 = f32[32,128]{1,0:T(8,128)} reduce(f32[16,32,128]{2,1,0:T(8,128)S(1)} %all_to_all.10, f32[]{:T(128)} %constant.0.clone.1), dimensions={0}, to_apply=%region_0.0 | reduce | flops 61440 | bytes 278532 | tf_op jit(solution)/shard_map/reduce_sum | solution.py:365
Async XLA Ops:
  1.4 16.7 %all-to-all-start = ((f32[16,32,128]{2,1,0:T(8,128)}), f32[16,32,128]{2,1,0:T(8,128)S(1)}, u32[]{:S(2)}, u32[]{:S(2)}) async-start(f32[16,32,128]{2,1,0:T(8,128)} %broadcast_in_dim.2), calls=%async_computation | async-start | bytes 524288 | tf_op jit(solution)/shard_map/all_to_all | solution.py:361
  9.4 8.7 %copy-start = (f32[2,512,512]{2,1,0:T(8,128)S(1)}, f32[2,512,512]{2,1,0:T(8,128)}, u32[]{:S(2)}) copy-start(f32[2,512,512]{2,1,0:T(8,128)} %boundary_ref.1) | copy-start | bytes 6291460
  9.4 8.7 %copy-start.1 = (s32[2,16]{1,0:T(2,128)S(1)}, s32[2,16]{1,0:T(2,128)}, u32[]{:S(2)}) copy-start(s32[2,16]{1,0:T(2,128)} %ids_ref.1) | copy-start | bytes 388
  9.4 8.7 %copy-start.2 = (s32[2]{0:T(128)S(1)}, s32[2]{0:T(128)}, u32[]{:S(2)}) copy-start(s32[2]{0:T(128)} %live_ref.1) | copy-start | bytes 28

commit v4 on v3

--- a/solution.py
+++ b/solution.py
@@ -97,80 +97,6 @@
     return results
 
 
-def prepare_kernel(factor_ref, inverse_ref, held, inv, inverse, sem, out_sem):
-    districts, size, _ = factor_ref.shape
-    steps = size // TILE
-    blocks = [(d, k) for k in range(steps) for d in range(districts)]
-    loads, stores = {}, []
-    for d, k in blocks:
-        at = (d, pl.ds(k * TILE, TILE), pl.ds(k * TILE, TILE))
-        loads[d, k] = pltpu.make_async_copy(
-            factor_ref.at[at], held.at[d * steps + k], sem.at[d * steps + k]
-        )
-        loads[d, k].start()
-    tiles = [(d * steps + k, t) for d, k in blocks for t in range(2)]
-
-    def tile_at(at, t, u):
-        return held[at, pl.ds(t * HALF, HALF), pl.ds(u * HALF, HALF)]
-
-    for first in range(0, len(tiles), BATCH):
-        batch = tiles[first : first + BATCH]
-        for at, t in batch:
-            if t == 0:
-                loads[at // steps, at % steps].wait()
-        diagonal = [tile_at(at, t, t) for at, t in batch]
-        packed = base_inverses(diagonal)
-        width = BASE
-        while width < HALF:
-            packed = doubled(diagonal, packed, width)
-            width *= 2
-        for (at, t), x in zip(batch, packed):
-            inv[2 * at + t] = x
-    for first in range(0, len(blocks), BATCH // 2):
-        group = [d * steps + k for d, k in blocks[first : first + BATCH // 2]]
-        pairs = [(split(inv[2 * at]), split(inv[2 * at + 1])) for at in group]
-        lefts = [dot3(split(tile_at(at, 1, 0)), top) for at, (top, _) in zip(group, pairs)]
-        lefts = [split(-dot3(bottom, split(x))) for x, (_, bottom) in zip(lefts, pairs)]
-        zero = jnp.zeros((HALF, HALF), BF)
-        for at, (top, bottom), left in zip(group, pairs, lefts):
-            for i in range(2):
-                inverse[at, i, :HALF, :HALF] = top[i]
-                inverse[at, i, :HALF, HALF:] = zero
-                inverse[at, i, HALF:, :HALF] = left[i]
-                inverse[at, i, HALF:, HALF:] = bottom[i]
-            stores.append(
-                pltpu.make_async_copy(inverse.at[at], inverse_ref.at[at], out_sem.at[at])
-            )
-            stores[-1].start()
-    for copy in stores:
-        copy.wait()
-
-
-def prepare(factor):
-    districts, size, _ = factor.shape
-    count = districts * (size // TILE)
-    blocks = (count, 2, TILE, TILE)
-    anywhere = pl.BlockSpec(memory_space=pltpu.HBM)
-    return pl.pallas_call(
-        prepare_kernel,
-        out_shape=jax.ShapeDtypeStruct(blocks, BF),
-        in_specs=[anywhere],
-        out_specs=anywhere,
-        scratch_shapes=[
-            pltpu.VMEM((count, TILE, TILE), F32),
-            pltpu.VMEM((count * 2, LANES, LANES), F32),
-            pltpu.VMEM(blocks, BF),
-            pltpu.SemaphoreType.DMA((count,)),
-            pltpu.SemaphoreType.DMA((count,)),
-        ],
-        compiler_params=pltpu.CompilerParams(vmem_limit_bytes=61 << 20),
-        cost_estimate=pl.CostEstimate(
-            flops=20 * 10**9, bytes_accessed=12 << 20, transcendentals=0
-        ),
-        name="prepare",
-    )(factor)
-
-
 def apply_kernel(
     ids_ref,
     live_ref,
@@ -178,53 +104,45 @@
     coupling_ref,
     factor_ref,
     boundary_ref,
-    inverse_ref,
     out_ref,
-    held,
+    inv,
+    inverse,
     high,
     low,
-    coupling,
-    inverse,
-    sem,
-    inv_sem,
-    cpl_sem,
 ):
     slots, cases, _ = gathered_ref.shape
     districts, size, faces = coupling_ref.shape
     steps = size // TILE
     per = LANES // BS
+    everyone = range(districts)
+
+    blocks = [(d, k) for k in range(steps) for d in everyone]
+
+    def tile_at(d, k, t, u):
+        top, left = k * TILE + t * HALF, k * TILE + u * HALF
+        return factor_ref[d, pl.ds(top, HALF), pl.ds(left, HALF)]
+
+    for first in range(0, len(blocks), BATCH // 2):
+        batch = blocks[first : first + BATCH // 2]
+        diagonal = [tile_at(d, k, t, t) for d, k in batch for t in range(2)]
+        packed = base_inverses(diagonal)
+        width = BASE
+        while width < HALF:
+            packed = doubled(diagonal, packed, width)
+            width *= 2
+        pairs = [(split(packed[2 * i]), split(packed[2 * i + 1])) for i in range(len(batch))]
+        lefts = [dot3(split(tile_at(*at, 1, 0)), top) for at, (top, _) in zip(batch, pairs)]
+        lefts = [split(-dot3(bottom, split(x))) for x, (_, bottom) in zip(lefts, pairs)]
+        zero = jnp.zeros((HALF, HALF), BF)
+        for (d, k), (top, bottom), left in zip(batch, pairs, lefts):
+            at = d * steps + k
+            for i in range(2):
+                inverse[at, i, :HALF, :HALF] = top[i]
+                inverse[at, i, :HALF, HALF:] = zero
+                inverse[at, i, HALF:, :HALF] = left[i]
+                inverse[at, i, HALF:, HALF:] = bottom[i]
+
     group = lax.broadcasted_iota(jnp.int32, (cases, LANES), 1) // BS
-
-    couplings = [
-        pltpu.make_async_copy(coupling_ref.at[d], coupling.at[d], cpl_sem.at[d])
-        for d in range(districts)
-    ]
-    stages = []
-    for k in range(steps):
-        copies = []
-        for d in range(districts):
-            at = d * steps + k
-            copies.append(
-                pltpu.make_async_copy(inverse_ref.at[at], inverse.at[at], inv_sem.at[at])
-            )
-            if k < steps - 1:
-                at = (d, pl.ds((k + 1) * TILE, size - (k + 1) * TILE), pl.ds(k * TILE, TILE))
-                copies.append(
-                    pltpu.make_async_copy(factor_ref.at[at], held.at[at], sem.at[d, k])
-                )
-        stages.append(copies)
-    stages[2] = sum(stages[2:], [])
-
-    def start(copies):
-        for copy in copies:
-            copy.start()
-
-    def wait(copies):
-        for copy in copies:
-            copy.wait()
-
-    start(couplings)
-    start(stages[0])
 
     def stack(a):
         return jnp.concatenate(split(a), axis=0)
@@ -245,17 +163,12 @@
             columns.append(acc)
         x = stack(jnp.concatenate(columns, axis=1))
         masked.append(x)
-    start(stages[1])
     for d in range(districts):
         parts = split(boundary_ref[d])
         total.append(fold(dot_t(masked[d], parts[0]) + dot_t(masked[d], parts[1])))
     for d in range(districts):
-        wait(couplings[d : d + 1])
-        if d == 0:
-            start(stages[2])
-        right = dot_t(masked[d], coupling[d])
+        right = dot_t(masked[d], coupling_ref[d])
         rest.append([fold(right[:, k * TILE : (k + 1) * TILE]) for k in range(steps)])
-    everyone = range(districts)
     forward = [[None] * steps for _ in everyone]
     pairs = {}
 
@@ -267,14 +180,12 @@
 
     def update(d, k, j):
         block = (d, slice(j * TILE, (j + 1) * TILE), slice(k * TILE, (k + 1) * TILE))
-        parts = split(held[block])
+        parts = split(factor_ref[block])
         high[block], low[block] = parts
         step = dot_t(pairs[d, k], parts[0]) + dot_t(pairs[d, k], parts[1])
         rest[d][j] = rest[d][j] - fold(step)
 
     for k in range(steps):
-        if k < 3:
-            wait(stages[k])
         for d in everyone:
             advance(d, k)
         for d in everyone:
@@ -296,7 +207,7 @@
         forward[d][j] = forward[d][j] - fold(step)
 
     def finish(d, k):
-        c = coupling[d, k * TILE : (k + 1) * TILE]
+        c = coupling_ref[d, k * TILE : (k + 1) * TILE]
         total[d] = total[d] - fold(dot(pairs[d, k], c))
 
     for k in reversed(range(steps)):
@@ -326,42 +237,54 @@
         out_ref[s] = acc
 
 
-def apply(ids, live, gathered, coupling, factor, boundary, inverse):
+def apply(ids, live, gathered, coupling, factor, boundary):
     districts, size, faces = coupling.shape
-    steps = size // TILE
+    count = districts * (size // TILE)
     scalar = pl.BlockSpec(memory_space=pltpu.SMEM)
     whole = pl.BlockSpec(memory_space=pltpu.VMEM)
-    anywhere = pl.BlockSpec(memory_space=pltpu.HBM)
     return pl.pallas_call(
         apply_kernel,
         out_shape=jax.ShapeDtypeStruct(gathered.shape, F32),
-        in_specs=[scalar, scalar, whole, anywhere, anywhere, whole, anywhere],
+        in_specs=[scalar, scalar] + [whole] * 4,
         out_specs=whole,
         scratch_shapes=[
-            pltpu.VMEM((districts, size, size - TILE), F32),
+            pltpu.VMEM((count * 2, LANES, LANES), F32),
+            pltpu.VMEM((count, 2, TILE, TILE), BF),
             pltpu.VMEM((districts, size, size - TILE), BF),
             pltpu.VMEM((districts, size, size - TILE), BF),
-            pltpu.VMEM(coupling.shape, BF),
-            pltpu.VMEM(inverse.shape, BF),
-            pltpu.SemaphoreType.DMA((districts, steps - 1)),
-            pltpu.SemaphoreType.DMA((districts * steps,)),
-            pltpu.SemaphoreType.DMA((districts,)),
         ],
-        compiler_params=pltpu.CompilerParams(vmem_limit_bytes=50 << 20),
+        compiler_params=pltpu.CompilerParams(vmem_limit_bytes=28 << 20),
         cost_estimate=pl.CostEstimate(
             flops=10 * 10**9, bytes_accessed=24 << 20, transcendentals=0
         ),
         name="apply",
-    )(ids, live, gathered, coupling, factor, boundary, inverse)
+    )(ids, live, gathered, coupling, factor, boundary)
+
+
+def pack_kernel(loads_ref, out_ref):
+    loads = loads_ref[...]
+    for p in range(out_ref.shape[0]):
+        out_ref[p] = loads
+
+
+def pack(loads, copies):
+    whole = pl.BlockSpec(memory_space=pltpu.VMEM)
+    return pl.pallas_call(
+        pack_kernel,
+        out_shape=jax.ShapeDtypeStruct((copies,) + loads.shape, F32),
+        in_specs=[whole],
+        out_specs=whole,
+        compiler_params=pltpu.CompilerParams(vmem_limit_bytes=2 << 20),
+        cost_estimate=pl.CostEstimate(
+            flops=30 * 10**9, bytes_accessed=1 << 20, transcendentals=0
+        ),
+        name="pack",
+    )(loads)
 
 
 def body(factor, coupling, boundary, loads, block_ids, live_counts):
-    cols = lax.axis_size("col")
-    send = jnp.broadcast_to(loads[None], (cols,) + loads.shape)
-    gathered = lax.all_to_all(send, "col", 0, 0)
-    back = apply(
-        block_ids, live_counts, gathered, coupling, factor, boundary, prepare(factor)
-    )
+    gathered = lax.all_to_all(pack(loads, lax.axis_size("col")), "col", 0, 0)
+    back = apply(block_ids, live_counts, gathered, coupling, factor, boundary)
     return jnp.sum(lax.all_to_all(back, "col", 0, 0), axis=0)
 
 

time: 45 us -> 41.6 us (0.924)
  blocking collectives: 14.5 us -> 28.3 us
  starting transfers between devices: 7.96 us -> 0 us
  Pallas kernels: 18.9 us -> 11.5 us
  waiting for transfers between devices: 1.24 us -> 0 us
  local copies, waits for them, and re-layouts: 1.46 us -> 0.89 us
    all_to_all x0 -> x1, blocking collectives: none -> 16.7 us  [body(): gathered = lax.all_to_all(pack(loads, lax.axis_size('col')), 'col', 0, 0)]
    all_to_all x1 -> x0, starting transfers between devices: 7.96 us -> none  [body(): gathered = lax.all_to_all(send, 'col', 0, 0)]
    pallas_call x1, Pallas kernels: 7.41 us -> 0.02 us  [pack(): pl.pallas_call(pack_kernel, out_shape=jax.ShapeDtypeStruct((copies,) + lo...]
    all_to_all x1, blocking collectives: 14.5 us -> 11.6 us  [body(): return jnp.sum(lax.all_to_all(back, 'col', 0, 0), axis=0)]
    broadcast_in_dim x1 -> x0, local copies, waits for them, and re-layouts: 1.44 us -> none  [body(): send = jnp.broadcast_to(loads[None], (cols,) + loads.shape)]
    all_to_all x1 -> x0, waiting for transfers between devices: 1.24 us -> none  [body(): gathered = lax.all_to_all(send, 'col', 0, 0)]
    unnamed x6 -> x12, local copies, waits for them, and re-layouts: 0.02 us -> 0.89 us
  transfers between devices with their start and end apart: 1 -> 0, of which waited for: 1 -> 0; matrix products, arithmetic and copies ran while one was open for 0% -> 0% of each run, Pallas kernels for 17% -> 0%
where the time goes in v4:
time: 41.6 us; the launch traced here: 41.4 us
  blocking collectives  28.3 us (68%)
  Pallas kernels  11.5 us (28%)
  local copies, waits for them, and re-layouts  0.89 us (2%)
  other arithmetic  0.63 us (2%)
    all_to_all x1, blocking collectives, body(): gathered = lax.all_to_all(pack(loads, lax.axis_size('col')), 'col', 0, 0)  16.7 us
    all_to_all x1, blocking collectives, body(): return jnp.sum(lax.all_to_all(back, 'col', 0, 0), axis=0)  11.6 us
    pallas_call x1, Pallas kernels, apply(): pl.pallas_call(apply_kernel, out_shape=jax.ShapeDtypeStruct(gathered.shap...  11.5 us
    unnamed x12, local copies, waits for them, and re-layouts  0.89 us

profile of v4, /device:TPU:0, one launch (start us, length us, event | category | flops | bytes accessed | tf_op | source)
XLA Modules:
  0.0 41.4 jit_solution(6085527876283771969)
XLA Ops:
  0.0 0.0 copy-start.2
  0.0 0.0 copy-start.1
  0.0 0.0 copy-start.3
  0.0 0.9 %copy-done.3 = f32[32,128]{1,0:T(8,128)S(1)} copy-done((f32[32,128]{1,0:T(8,128)S(1)}, f32[32,128]{1,0:T(8,128)}, u32[]{:S(2)}) %copy-start.3) | copy-done | bytes 16408
  0.9 0.0 copy-start
  0.9 0.0 copy-start.4
  0.9 0.0 copy-start.5
  0.9 16.7 %all_to_all.10.gathered_ref = f32[16,32,128]{2,1,0:T(8,128)S(1)} all-to-all(f32[16,32,128]{2,1,0:T(8,128)S(1)} %pack.1), channel_id=1, replica_groups=mesh['row'=8,'col'=16] {'col'}, dimensions={0} | all-to-all | bytes 524288 | tf_op jit(solution)/shard_map/all_to_all | solution.py:286
  17.6 0.0 copy-done.2
  17.6 0.0 copy-done.1
  17.6 0.0 copy-done
  17.6 0.0 copy-done.4
  17.6 0.0 copy-done.5
  17.7 11.5 %apply.1 = f32[16,32,128]{2,1,0:T(8,128)S(1)} custom-call(s32[2,16]{1,0:T(2,128)S(1)} %copy-done.4, s32[2]{0:T(128)S(1)} %copy-done.5, f32[16,32,128]{2,1,0:T(8,128)S(1)} %all_to_all.10.gathered_ref, bf16[2,1536,512]{2,1,0:T(8,128)(2,1)S(1)} %copy-done.1, f32[2,1536,1536]{2,1,0:T(8,128)S(1)} %copy-done, f32[2,512,512]{2,1,0:T(8,128)S(1)} %copy-done.2), custom_call_target="tpu_custom_call" | custom-call | flops 10000000000 | bytes 25165824 | tf_op jit(solution)/shard_map/apply/pallas_call | solution.py:245
  29.2 11.6 %all_to_all.11 = f32[16,32,128]{2,1,0:T(8,128)S(1)} all-to-all(f32[16,32,128]{2,1,0:T(8,128)S(1)} %apply.1), channel_id=1, replica_groups=mesh['row'=8,'col'=16] {'col'}, dimensions={0} | all-to-all | bytes 524288 | tf_op jit(solution)/shard_map/all_to_all | solution.py:288
  40.8 0.6 %reduce_sum.9 = f32[32,128]{1,0:T(8,128)} reduce(f32[16,32,128]{2,1,0:T(8,128)S(1)} %all_to_all.11, f32[]{:T(128)} %constant.0.clone.1), dimensions={0}, to_apply=%region_0.0 | reduce | flops 61440 | bytes 278532 | tf_op jit(solution)/shard_map/reduce_sum | solution.py:288
  (1 shorter events, 0.0 us)
Async XLA Ops:
  0.0 17.6 %copy-start.2 = (f32[2,512,512]{2,1,0:T(8,128)S(1)}, f32[2,512,512]{2,1,0:T(8,128)}, u32[]{:S(2)}) copy-start(f32[2,512,512]{2,1,0:T(8,128)} %boundary_ref.1) | copy-start | bytes 6291460
  0.0 17.6 %copy-start.1 = (bf16[2,1536,512]{2,1,0:T(8,128)(2,1)S(1)}, bf16[2,1536,512]{2,1,0:T(8,128)(2,1)}, u32[]{:S(2)}) copy-start(bf16[2,1536,512]{2,1,0:T(8,128)(2,1)} %coupling_ref.1) | copy-start | bytes 9437188
  0.0 0.9 %copy-start.3 = (f32[32,128]{1,0:T(8,128)S(1)}, f32[32,128]{1,0:T(8,128)}, u32[]{:S(2)}) copy-start(f32[32,128]{1,0:T(8,128)} %loads_ref.1) | copy-start | bytes 49156
  0.9 16.8 %copy-start = (f32[2,1536,1536]{2,1,0:T(8,128)S(1)}, f32[2,1536,1536]{2,1,0:T(8,128)}, u32[]{:S(2)}) copy-start(f32[2,1536,1536]{2,1,0:T(8,128)} %factor_ref.1) | copy-start | bytes 56623108
  0.9 16.8 %copy-start.4 = (s32[2,16]{1,0:T(2,128)S(1)}, s32[2,16]{1,0:T(2,128)}, u32[]{:S(2)}) copy-start(s32[2,16]{1,0:T(2,128)} %ids_ref.1) | copy-start | bytes 388
  0.9 16.8 %copy-start.5 = (s32[2]{0:T(128)S(1)}, s32[2]{0:T(128)}, u32[]{:S(2)}) copy-start(s32[2]{0:T(128)} %live_ref.1) | copy-start | bytes 28

commit v5 on v4

--- a/solution.py
+++ b/solution.py
@@ -49,6 +49,7 @@
         acc = jnp.where(row == column, 1.0, 0.0).astype(F32)
         states.append([acc[8 * g : 8 * g + 8] for g in range(BASE // 8)])
     for j in range(BASE - 1):
+        yield
         index = group[:8] * BASE + j
         for unit, parts in zip(units, states):
             pivot = parts[j // 8][j % 8 : j % 8 + 1]
@@ -62,6 +63,16 @@
         )
         results.append(jnp.concatenate(parts, axis=0) * scale)
     return results
+
+
+def together(*tasks):
+    tasks = [list(task) for task in tasks]
+    while tasks:
+        for task in list(tasks):
+            for _ in range(task[1]):
+                if next(task[0], tasks) is tasks:
+                    tasks.remove(task)
+                    break
 
 
 def doubled(tiles, packed, width):
@@ -81,6 +92,7 @@
         ]
         product = dot(jnp.concatenate([below, below], axis=1), jnp.concatenate(spread, axis=0))
         products.append(product[:width] + product[width:])
+    yield
     results = []
     for x, product in zip(packed, products):
         odd = jnp.concatenate(split(jnp.where(even, 0.0, x)), axis=0)
@@ -122,17 +134,20 @@
         top, left = k * TILE + t * HALF, k * TILE + u * HALF
         return factor_ref[d, pl.ds(top, HALF), pl.ds(left, HALF)]
 
-    for first in range(0, len(blocks), BATCH // 2):
-        batch = blocks[first : first + BATCH // 2]
+    def invert(batch):
         diagonal = [tile_at(d, k, t, t) for d, k in batch for t in range(2)]
-        packed = base_inverses(diagonal)
+        packed = yield from base_inverses(diagonal)
         width = BASE
         while width < HALF:
-            packed = doubled(diagonal, packed, width)
+            yield
+            packed = yield from doubled(diagonal, packed, width)
             width *= 2
         pairs = [(split(packed[2 * i]), split(packed[2 * i + 1])) for i in range(len(batch))]
+        yield
         lefts = [dot3(split(tile_at(*at, 1, 0)), top) for at, (top, _) in zip(batch, pairs)]
+        yield
         lefts = [split(-dot3(bottom, split(x))) for x, (_, bottom) in zip(lefts, pairs)]
+        yield
         zero = jnp.zeros((HALF, HALF), BF)
         for (d, k), (top, bottom), left in zip(batch, pairs, lefts):
             at = d * steps + k
@@ -150,25 +165,35 @@
     def fold(a):
         return a[:cases] + a[cases:]
 
-    masked, total, rest = [], [], []
-    for d in range(districts):
-        columns = []
-        for tile in range(slots // per):
-            acc = jnp.zeros((cases, LANES), F32)
-            for g in range(per):
-                s = tile * per + g
-                within = ids_ref[d, s] % per
-                piece = pltpu.roll(gathered_ref[s], ((g + per - within) % per) * BS, 1)
-                acc = jnp.where((group == g) & (s < live_ref[d]), piece, acc)
-            columns.append(acc)
-        x = stack(jnp.concatenate(columns, axis=1))
-        masked.append(x)
-    for d in range(districts):
-        parts = split(boundary_ref[d])
-        total.append(fold(dot_t(masked[d], parts[0]) + dot_t(masked[d], parts[1])))
-    for d in range(districts):
-        right = dot_t(masked[d], coupling_ref[d])
-        rest.append([fold(right[:, k * TILE : (k + 1) * TILE]) for k in range(steps)])
+    masked = []
+    total, rest = [[] for _ in everyone], [[] for _ in everyone]
+    def gather():
+        for d in everyone:
+            columns = []
+            for tile in range(slots // per):
+                acc = jnp.zeros((cases, LANES), F32)
+                for g in range(per):
+                    s = tile * per + g
+                    within = ids_ref[d, s] % per
+                    piece = pltpu.roll(gathered_ref[s], ((g + per - within) % per) * BS, 1)
+                    acc = jnp.where((group == g) & (s < live_ref[d]), piece, acc)
+                columns.append(acc)
+            masked.append(stack(jnp.concatenate(columns, axis=1)))
+        for k in range(steps):
+            for d in everyone:
+                yield
+                right = dot_t(masked[d], coupling_ref[d, k * TILE : (k + 1) * TILE])
+                rest[d].append(fold(right))
+
+    def direct():
+        for part in range(faces // LANES):
+            for d in everyone:
+                yield
+                rows = slice(part * LANES, (part + 1) * LANES)
+                parts = split(boundary_ref[d, rows])
+                image = dot_t(masked[d], parts[0]) + dot_t(masked[d], parts[1])
+                total[d].append(fold(image))
+
     forward = [[None] * steps for _ in everyone]
     pairs = {}
 
@@ -182,19 +207,30 @@
         block = (d, slice(j * TILE, (j + 1) * TILE), slice(k * TILE, (k + 1) * TILE))
         parts = split(factor_ref[block])
         high[block], low[block] = parts
-        step = dot_t(pairs[d, k], parts[0]) + dot_t(pairs[d, k], parts[1])
+        turned = split(factor_ref[block].T)
+        step = dot(pairs[d, k], turned[0]) + dot(pairs[d, k], turned[1])
         rest[d][j] = rest[d][j] - fold(step)
 
-    for k in range(steps):
-        for d in everyone:
-            advance(d, k)
-        for d in everyone:
-            if d == 1 and k + 1 < steps:
-                for e in everyone:
-                    update(e, k, k + 1)
-            if k > 0:
-                for j in range(k + 1, steps):
-                    update(d, k - 1, j)
+    def solve(first, last):
+        for k in range(first, last):
+            for d in everyone:
+                advance(d, k)
+                yield
+            for d in everyone:
+                if d == 1 and k + 1 < steps:
+                    for e in everyone:
+                        update(e, k, k + 1)
+                        yield
+                if k > 0:
+                    for j in range(k + 1, steps):
+                        update(d, k - 1, j)
+                        yield
+
+    half = len(blocks) // 3
+    together((invert(blocks[:half]), 1), (gather(), 1))
+    together((invert(blocks[half:]), 1), (solve(0, 2), 1))
+    together((solve(2, steps), 1), (direct(), 1))
+    total = [jnp.concatenate(halves, axis=1) for halves in total]
 
     def retreat(d, k):
         at = d * steps + k

time: 41.6 us -> 40.5 us (0.974)
  Pallas kernels: 11.5 us -> 10.4 us
    pallas_call x1, Pallas kernels: 11.5 us -> 10.4 us  [apply(): pl.pallas_call(apply_kernel, out_shape=jax.ShapeDtypeStruct(gathered.shap...]
where the time goes in v5:
time: 40.5 us; the launch traced here: 40.3 us
  blocking collectives  28.3 us (70%)
  Pallas kernels  10.4 us (26%)
  local copies, waits for them, and re-layouts  0.89 us (2%)
  other arithmetic  0.63 us (2%)
    all_to_all x1, blocking collectives, body(): gathered = lax.all_to_all(pack(loads, lax.axis_size('col')), 'col', 0, 0)  16.7 us
    all_to_all x1, blocking collectives, body(): return jnp.sum(lax.all_to_all(back, 'col', 0, 0), axis=0)  11.6 us
    pallas_call x1, Pallas kernels, apply(): pl.pallas_call(apply_kernel, out_shape=jax.ShapeDtypeStruct(gathered.shap...  10.4 us
    unnamed x12, local copies, waits for them, and re-layouts  0.89 us

profile of v5, /device:TPU:0, one launch (start us, length us, event | category | flops | bytes accessed | tf_op | source)
XLA Modules:
  0.0 40.3 jit_solution(8636423572461236530)
XLA Ops:
  0.0 0.0 copy-start.2
  0.0 0.0 copy-start.1
  0.0 0.0 copy-start.3
  0.0 0.9 %copy-done.3 = f32[32,128]{1,0:T(8,128)S(1)} copy-done((f32[32,128]{1,0:T(8,128)S(1)}, f32[32,128]{1,0:T(8,128)}, u32[]{:S(2)}) %copy-start.3) | copy-done | bytes 16408
  0.9 0.0 copy-start
  0.9 0.0 copy-start.4
  0.9 0.0 copy-start.5
  0.9 16.7 %all_to_all.10.gathered_ref = f32[16,32,128]{2,1,0:T(8,128)S(1)} all-to-all(f32[16,32,128]{2,1,0:T(8,128)S(1)} %pack.1), channel_id=1, replica_groups=mesh['row'=8,'col'=16] {'col'}, dimensions={0} | all-to-all | bytes 524288 | tf_op jit(solution)/shard_map/all_to_all | solution.py:322
  17.6 0.0 copy-done.2
  17.6 0.0 copy-done.1
  17.6 0.0 copy-done
  17.6 0.0 copy-done.4
  17.6 0.0 copy-done.5
  17.7 10.4 %apply.1 = f32[16,32,128]{2,1,0:T(8,128)S(1)} custom-call(s32[2,16]{1,0:T(2,128)S(1)} %copy-done.4, s32[2]{0:T(128)S(1)} %copy-done.5, f32[16,32,128]{2,1,0:T(8,128)S(1)} %all_to_all.10.gathered_ref, bf16[2,1536,512]{2,1,0:T(8,128)(2,1)S(1)} %copy-done.1, f32[2,1536,1536]{2,1,0:T(8,128)S(1)} %copy-done, f32[2,512,512]{2,1,0:T(8,128)S(1)} %copy-done.2), custom_call_target="tpu_custom_call" | custom-call | flops 10000000000 | bytes 25165824 | tf_op jit(solution)/shard_map/apply/pallas_call | solution.py:281
  28.1 11.6 %all_to_all.11 = f32[16,32,128]{2,1,0:T(8,128)S(1)} all-to-all(f32[16,32,128]{2,1,0:T(8,128)S(1)} %apply.1), channel_id=1, replica_groups=mesh['row'=8,'col'=16] {'col'}, dimensions={0} | all-to-all | bytes 524288 | tf_op jit(solution)/shard_map/all_to_all | solution.py:324
  39.6 0.6 %reduce_sum.9 = f32[32,128]{1,0:T(8,128)} reduce(f32[16,32,128]{2,1,0:T(8,128)S(1)} %all_to_all.11, f32[]{:T(128)} %constant.0.clone.1), dimensions={0}, to_apply=%region_0.0 | reduce | flops 61440 | bytes 278532 | tf_op jit(solution)/shard_map/reduce_sum | solution.py:324
  (1 shorter events, 0.0 us)
Async XLA Ops:
  0.0 17.6 %copy-start.2 = (f32[2,512,512]{2,1,0:T(8,128)S(1)}, f32[2,512,512]{2,1,0:T(8,128)}, u32[]{:S(2)}) copy-start(f32[2,512,512]{2,1,0:T(8,128)} %boundary_ref.1) | copy-start | bytes 6291460
  0.0 17.6 %copy-start.1 = (bf16[2,1536,512]{2,1,0:T(8,128)(2,1)S(1)}, bf16[2,1536,512]{2,1,0:T(8,128)(2,1)}, u32[]{:S(2)}) copy-start(bf16[2,1536,512]{2,1,0:T(8,128)(2,1)} %coupling_ref.1) | copy-start | bytes 9437188
  0.0 0.9 %copy-start.3 = (f32[32,128]{1,0:T(8,128)S(1)}, f32[32,128]{1,0:T(8,128)}, u32[]{:S(2)}) copy-start(f32[32,128]{1,0:T(8,128)} %loads_ref.1) | copy-start | bytes 49156
  0.9 16.8 %copy-start = (f32[2,1536,1536]{2,1,0:T(8,128)S(1)}, f32[2,1536,1536]{2,1,0:T(8,128)}, u32[]{:S(2)}) copy-start(f32[2,1536,1536]{2,1,0:T(8,128)} %factor_ref.1) | copy-start | bytes 56623108
  0.9 16.8 %copy-start.4 = (s32[2,16]{1,0:T(2,128)S(1)}, s32[2,16]{1,0:T(2,128)}, u32[]{:S(2)}) copy-start(s32[2,16]{1,0:T(2,128)} %ids_ref.1) | copy-start | bytes 388
  0.9 16.8 %copy-start.5 = (s32[2]{0:T(128)S(1)}, s32[2]{0:T(128)}, u32[]{:S(2)}) copy-start(s32[2]{0:T(128)} %live_ref.1) | copy-start | bytes 28

commit v6 on v5

--- a/solution.py
+++ b/solution.py
@@ -229,9 +229,6 @@
     half = len(blocks) // 3
     together((invert(blocks[:half]), 1), (gather(), 1))
     together((invert(blocks[half:]), 1), (solve(0, 2), 1))
-    together((solve(2, steps), 1), (direct(), 1))
-    total = [jnp.concatenate(halves, axis=1) for halves in total]
-
     def retreat(d, k):
         at = d * steps + k
         r = stack(forward[d][k])
@@ -244,21 +241,38 @@
 
     def finish(d, k):
         c = coupling_ref[d, k * TILE : (k + 1) * TILE]
-        total[d] = total[d] - fold(dot(pairs[d, k], c))
-
-    for k in reversed(range(steps)):
+        image = fold(dot(pairs[d, k], c))
+        minus[d] = image if minus[d] is None else minus[d] + image
+
+    minus = [None] * districts
+
+    def solve_back():
+        for k in reversed(range(steps)):
+            for d in everyone:
+                retreat(d, k)
+                yield
+            for d in everyone:
+                if d == 1 and k > 0:
+                    for e in everyone:
+                        downdate(e, k, k - 1)
+                        yield
+                if k + 1 < steps:
+                    finish(d, k + 1)
+                    yield
+                    for j in reversed(range(k)):
+                        downdate(d, k + 1, j)
+                        yield
         for d in everyone:
-            retreat(d, k)
-        for d in everyone:
-            if d == 1 and k > 0:
-                for e in everyone:
-                    downdate(e, k, k - 1)
-            if k + 1 < steps:
-                finish(d, k + 1)
-                for j in reversed(range(k)):
-                    downdate(d, k + 1, j)
-    for d in everyone:
-        finish(d, 0)
+            finish(d, 0)
+            yield
+
+    def both():
+        yield from solve(steps - 2, steps)
+        yield from solve_back()
+
+    together((solve(2, steps - 2), 1))
+    together((both(), 1), (direct(), 1))
+    total = [jnp.concatenate(halves, axis=1) - m for halves, m in zip(total, minus)]
     for s in range(slots):
         acc = jnp.zeros((cases, LANES), F32)
         for d in range(districts):

time: 40.5 us -> 40.2 us (level)
  no operation moved by 1% of the time
where the time goes in v6:
time: 40.2 us; the launch traced here: 39.9 us
  blocking collectives  28.3 us (70%)
  Pallas kernels  10.1 us (25%)
  local copies, waits for them, and re-layouts  0.89 us (2%)
  other arithmetic  0.63 us (2%)
    all_to_all x1, blocking collectives, body(): gathered = lax.all_to_all(pack(loads, lax.axis_size('col')), 'col', 0, 0)  16.7 us
    all_to_all x1, blocking collectives, body(): return jnp.sum(lax.all_to_all(back, 'col', 0, 0), axis=0)  11.6 us
    pallas_call x1, Pallas kernels, apply(): pl.pallas_call(apply_kernel, out_shape=jax.ShapeDtypeStruct(gathered.shap...  10.1 us
    unnamed x12, local copies, waits for them, and re-layouts  0.89 us

profile of v6, /device:TPU:0, one launch (start us, length us, event | category | flops | bytes accessed | tf_op | source)
XLA Modules:
  0.0 39.9 jit_solution(11419014409200565667)
XLA Ops:
  0.0 0.0 copy-start.2
  0.0 0.0 copy-start.1
  0.0 0.0 copy-start.3
  0.0 0.9 %copy-done.3 = f32[32,128]{1,0:T(8,128)S(1)} copy-done((f32[32,128]{1,0:T(8,128)S(1)}, f32[32,128]{1,0:T(8,128)}, u32[]{:S(2)}) %copy-start.3) | copy-done | bytes 16408
  0.9 0.0 copy-start
  0.9 0.0 copy-start.4
  0.9 0.0 copy-start.5
  0.9 16.7 %all_to_all.10.gathered_ref = f32[16,32,128]{2,1,0:T(8,128)S(1)} all-to-all(f32[16,32,128]{2,1,0:T(8,128)S(1)} %pack.1), channel_id=1, replica_groups=mesh['row'=8,'col'=16] {'col'}, dimensions={0} | all-to-all | bytes 524288 | tf_op jit(solution)/shard_map/all_to_all | solution.py:336
  17.6 0.0 copy-done.2
  17.6 0.0 copy-done.1
  17.6 0.0 copy-done
  17.6 0.0 copy-done.4
  17.6 0.0 copy-done.5
  17.7 10.1 %apply.1 = f32[16,32,128]{2,1,0:T(8,128)S(1)} custom-call(s32[2,16]{1,0:T(2,128)S(1)} %copy-done.4, s32[2]{0:T(128)S(1)} %copy-done.5, f32[16,32,128]{2,1,0:T(8,128)S(1)} %all_to_all.10.gathered_ref, bf16[2,1536,512]{2,1,0:T(8,128)(2,1)S(1)} %copy-done.1, f32[2,1536,1536]{2,1,0:T(8,128)S(1)} %copy-done, f32[2,512,512]{2,1,0:T(8,128)S(1)} %copy-done.2), custom_call_target="tpu_custom_call" | custom-call | flops 10000000000 | bytes 25165824 | tf_op jit(solution)/shard_map/apply/pallas_call | solution.py:295
  27.7 11.6 %all_to_all.11 = f32[16,32,128]{2,1,0:T(8,128)S(1)} all-to-all(f32[16,32,128]{2,1,0:T(8,128)S(1)} %apply.1), channel_id=1, replica_groups=mesh['row'=8,'col'=16] {'col'}, dimensions={0} | all-to-all | bytes 524288 | tf_op jit(solution)/shard_map/all_to_all | solution.py:338
  39.3 0.6 %reduce_sum.9 = f32[32,128]{1,0:T(8,128)} reduce(f32[16,32,128]{2,1,0:T(8,128)S(1)} %all_to_all.11, f32[]{:T(128)} %constant.0.clone.1), dimensions={0}, to_apply=%region_0.0 | reduce | flops 61440 | bytes 278532 | tf_op jit(solution)/shard_map/reduce_sum | solution.py:338
  (1 shorter events, 0.0 us)
Async XLA Ops:
  0.0 17.6 %copy-start.2 = (f32[2,512,512]{2,1,0:T(8,128)S(1)}, f32[2,512,512]{2,1,0:T(8,128)}, u32[]{:S(2)}) copy-start(f32[2,512,512]{2,1,0:T(8,128)} %boundary_ref.1) | copy-start | bytes 6291460
  0.0 17.6 %copy-start.1 = (bf16[2,1536,512]{2,1,0:T(8,128)(2,1)S(1)}, bf16[2,1536,512]{2,1,0:T(8,128)(2,1)}, u32[]{:S(2)}) copy-start(bf16[2,1536,512]{2,1,0:T(8,128)(2,1)} %coupling_ref.1) | copy-start | bytes 9437188
  0.0 0.9 %copy-start.3 = (f32[32,128]{1,0:T(8,128)S(1)}, f32[32,128]{1,0:T(8,128)}, u32[]{:S(2)}) copy-start(f32[32,128]{1,0:T(8,128)} %loads_ref.1) | copy-start | bytes 49156
  0.9 16.8 %copy-start = (f32[2,1536,1536]{2,1,0:T(8,128)S(1)}, f32[2,1536,1536]{2,1,0:T(8,128)}, u32[]{:S(2)}) copy-start(f32[2,1536,1536]{2,1,0:T(8,128)} %factor_ref.1) | copy-start | bytes 56623108
  0.9 16.8 %copy-start.4 = (s32[2,16]{1,0:T(2,128)S(1)}, s32[2,16]{1,0:T(2,128)}, u32[]{:S(2)}) copy-start(s32[2,16]{1,0:T(2,128)} %ids_ref.1) | copy-start | bytes 388
  0.9 16.8 %copy-start.5 = (s32[2]{0:T(128)S(1)}, s32[2]{0:T(128)}, u32[]{:S(2)}) copy-start(s32[2]{0:T(128)} %live_ref.1) | copy-start | bytes 28
